TPU v7x, 128 devices: a whole 4x4x4 slice. The times are simulated.
128 devices in a mesh: ctx: 32 (over y, x, core), head: 4 (over z).
Axes of the slice: x: 4, y: 4, z: 4, core: 2. Of those that a mesh axis runs over, the one named last changes fastest.
Arguments:
- q_lin: float32 [8192, 4096], P('ctx', 'head'), may hold values from -6 to 6
- k_lin: float32 [8192, 4096], P('ctx', 'head'), may hold values from -0.9722718 to 0.9722718
- v_lin: float32 [8192, 4096], P('ctx', 'head'), may hold values from -201 to 201
- log_decay: float32 [32, 8192], P('head', 'ctx'), may hold values from -1 to 0
- lin_gain: float32 [4096], P('head'), may hold values from 0.1 to 1.9
- q_soft: float32 [8192, 6144], P('ctx', 'head'), may hold values from -36 to 36
- k_soft: float32 [8192, 1024], P('ctx', 'head'), may hold values from -4 to 4
- v_soft: float32 [8192, 1024], P('ctx', 'head'), may hold values from -6 to 6
Outputs:
- lin_out: float32 [8192, 4096], P('ctx', 'head')
- soft_out: float32 [8192, 6144], P('ctx', 'head')
All inputs are finite; a program needn't handle non-finite values.
Results may differ from a plain program's by a relative error of at most 0.0003.
Values sent between devices are 32-bit elements; how exact they have to be, the bound alone decides.
A program may use at most 128 MiB of HBM per device.

v0:
```python
import math
import jax
import jax.numpy as jnp
from jax import lax
from jax.sharding import PartitionSpec as P

HD = 128
LH = 32
HIGHEST = lax.Precision.HIGHEST
NEGATIVE = -1e30
EPSILON = 1e-05


def entering(value, axis, combine, identity):
    count, mine = (lax.axis_size(axis), lax.axis_index(axis))
    everything = jax.tree.map(lambda part: lax.all_gather(part, axis), value)
    start = jax.tree.map(
        lambda part, zero: jnp.broadcast_to(jnp.asarray(zero, part.dtype), part.shape),
        value,
        identity,
    )

    def turn(k, before):
        reached = k < mine
        new = combine(before, jax.tree.map(lambda part: part[k], everything))
        return jax.tree.map(lambda a, b: jnp.where(reached, a, b), new, before)

    return lax.fori_loop(0, count, turn, start)


def block_terms(queries, key_rows, value_rows, log_rates):
    length = queries.shape[0]
    cumulative = jnp.cumsum(log_rates, axis=1)
    positions = jnp.arange(length)
    causal = (positions[:, None] >= positions[None, :])[None]
    decay_gaps = cumulative[:, :, None] - cumulative[:, None, :]
    weights = jnp.where(causal, jnp.exp(jnp.where(causal, decay_gaps, 0.0)), 0.0)
    scores = jnp.einsum("thd,shd->hts", queries, key_rows, precision=HIGHEST)
    inside = jnp.einsum("hts,shd->thd", scores * weights, value_rows, precision=HIGHEST)
    block_total = cumulative[:, -1]
    trailing = jnp.exp(block_total[:, None] - cumulative)
    scaled_keys = key_rows * jnp.transpose(trailing)[:, :, None]
    local_state = jnp.einsum("shd,she->hde", scaled_keys, value_rows, precision=HIGHEST)
    leading = jnp.transpose(jnp.exp(cumulative))[:, :, None]
    return (inside, leading, block_total, local_state)


def attend(partial_value, query_rows, query_pos, key_slab, value_slab, key_pos, score_scale):
    old_max, old_total, weighted = partial_value
    scores = jnp.einsum("tkgd,skd->kgts", query_rows, key_slab, precision=HIGHEST) * score_scale
    visible = (key_pos[None, :] <= query_pos[:, None])[None, None]
    scores = jnp.where(visible, scores, NEGATIVE)
    new_max = jnp.maximum(old_max, jnp.max(scores, axis=3))
    weights = jnp.where(visible, jnp.exp(scores - new_max[..., None]), 0.0)
    shrink = jnp.exp(old_max - new_max)
    new_total = old_total * shrink + jnp.sum(weights, axis=3)
    weighted = weighted * shrink[..., None] + jnp.einsum(
        "kgts,skd->kgtd", weights, value_slab, precision=HIGHEST
    )
    return (new_max, new_total, weighted)


def soft_layer(query_sets, k_soft, v_soft, score_scale):
    kv_heads = k_soft.shape[1] // HD
    initial = []
    for query_rows, query_pos in query_sets:
        shape = (query_rows.shape[1], query_rows.shape[2], query_rows.shape[0])
        initial.append(
            (
                jnp.full(shape, NEGATIVE, jnp.float32),
                jnp.zeros(shape, jnp.float32),
                jnp.zeros(shape + (HD,), jnp.float32),
            )
        )
    initial = tuple(initial)
    key_rows = lax.all_gather(k_soft, "ctx", axis=0, tiled=True)
    value_rows = lax.all_gather(v_soft, "ctx", axis=0, tiled=True)
    shard_rows = key_rows.shape[0]
    key_block = math.gcd(shard_rows, 512)
    key_rows = key_rows.reshape(shard_rows // key_block, key_block, kv_heads, HD)
    value_rows = value_rows.reshape(shard_rows // key_block, key_block, kv_heads, HD)

    def visit(block_index, partials):
        key_slab = lax.dynamic_index_in_dim(key_rows, block_index, 0, keepdims=False)
        value_slab = lax.dynamic_index_in_dim(value_rows, block_index, 0, keepdims=False)
        first_key = block_index * key_block
        key_pos = first_key + jnp.arange(key_block)
        updated = []
        for (query_rows, query_pos), partial_value in zip(query_sets, partials):

            def engage(current, query_rows=query_rows, query_pos=query_pos):
                return attend(
                    current, query_rows, query_pos, key_slab, value_slab, key_pos, score_scale
                )

            def remain(current):
                return current

            updated.append(lax.cond(first_key <= jnp.max(query_pos), engage, remain, partial_value))
        return tuple(updated)

    finals = lax.fori_loop(0, shard_rows // key_block, visit, initial)
    results = []
    for final in finals:
        maxima, totals, weighted = final
        merged = weighted / totals[..., None]
        row_count = merged.shape[2]
        results.append(jnp.transpose(merged, (2, 0, 1, 3)).reshape(row_count, -1))
    return results


def body(q_lin, k_lin, v_lin, log_decay, lin_gain, q_soft, k_soft, v_soft):
    row_count = q_lin.shape[0]
    head_count = log_decay.shape[0]
    position = lax.axis_index("ctx")
    queries = q_lin.reshape(row_count, head_count, HD)
    key_rows = k_lin.reshape(row_count, head_count, HD)
    value_rows = v_lin.reshape(row_count, head_count, HD)
    inside, leading, block_total, local_state = block_terms(
        queries, key_rows, value_rows, log_decay
    )

    def chain_step(earlier, later):
        return (earlier[0] + later[0], jnp.exp(later[0])[:, None, None] * earlier[1] + later[1])

    identity = (jnp.zeros_like(block_total), jnp.zeros_like(local_state))
    prefix_pair = entering((block_total, local_state), "ctx", chain_step, identity)
    prior_state = prefix_pair[1]
    linear = inside + leading * jnp.einsum("thd,hde->the", queries, prior_state, precision=HIGHEST)
    linear = linear.reshape(row_count, head_count * HD)
    energy = lax.psum(jnp.sum(linear * linear, axis=1, keepdims=True), "head")
    lin_out = linear * lax.rsqrt(energy / (LH * HD) + EPSILON) * lin_gain
    score_scale = 1.0 / math.sqrt(HD)
    kv_heads = k_soft.shape[1] // HD
    group_size = q_soft.shape[1] // (kv_heads * HD)
    soft_queries = q_soft.reshape(row_count, kv_heads, group_size, HD)
    query_pos = position * row_count + jnp.arange(row_count)
    soft_out = soft_layer([(soft_queries, query_pos)], k_soft, v_soft, score_scale)[0]
    return (lin_out, soft_out)


def solution(mesh):
    return jax.shard_map(
        body,
        mesh=mesh,
        in_specs=(
            P("ctx", "head"),
            P("ctx", "head"),
            P("ctx", "head"),
            P("head", "ctx"),
            P("head"),
            P("ctx", "head"),
            P("ctx", "head"),
            P("ctx", "head"),
        ),
        out_specs=(P("ctx", "head"), P("ctx", "head")),
        check_vma=False,
    )
```

profile of v0, /device:TPU:30, one launch (start us, length us, event | category | flops | bytes accessed | tf_op | source)
XLA Modules:
  0.0 573.1 jit_solution(4927016760311225648)
XLA Ops:
  17.5 59.2 %all-reduce = f32[256]{0:T(256)S(1)} all-reduce(f32[256]{0:T(256)S(1)} %dynamic-update-slice), channel_id=2, replica_groups=mesh['ctx'=32,'head'=4] {'ctx'}, use_global_device_ids=true, to_apply=%add | all-reduce | flops 256 | bytes 2048
  86.8 10.8 %reshape.135 = f32[16,512,2,128]{3,2,1,0:T(2,128)} reshape(f32[8192,256]{1,0:T(8,128)} %all-gather.6.cloned.1.call-done) | data formatting | bytes 16777216 | tf_op jit(solution)/shard_map/reshape | solution.py:80
  97.6 8.1 %copy.66 = f32[16,512,2,128]{3,1,2,0:T(8,128)} copy(f32[16,512,2,128]{3,2,1,0:T(2,128)} %reshape.135) | data formatting | bytes 16777216
  105.7 12.2 %all-gather.8.cloned.1.call-done = f32[8192,256]{1,0:T(8,128)} async-done(((f32[256,256]{1,0:T(8,128)}), f32[8192,256]{1,0:T(8,128)}) %all-gather.8.cloned.1.call-update) | async-done | bytes 8388624 | tf_op jit(solution)/shard_map/all_gather | solution.py:77
  117.9 10.8 %reshape.136 = f32[16,512,2,128]{3,2,1,0:T(2,128)} reshape(f32[8192,256]{1,0:T(8,128)} %all-gather.8.cloned.1.call-done) | data formatting | bytes 16777216 | tf_op jit(solution)/shard_map/reshape | solution.py:81
  128.7 7.9 %copy.68 = f32[16,512,2,128]{3,1,2,0:T(8,128)} copy(f32[16,512,2,128]{3,2,1,0:T(2,128)} %reshape.136) | data formatting | bytes 16777216
  137.9 363.9 %while.33 = (s32[]{:T(128)}, f32[2,6,256]{2,1,0:T(8,128)S(1)}, f32[2,6,256]{2,1,0:T(8,128)S(1)}, f32[2,6,256,128]{3,2,1,0:T(8,128)}, s32[]{:T(128)}, /*index=5*/...) while((s32[]{:T(128)}, f32[2,6,256]{2,1,0:T(8,128)S(1)}, ...), condition=%wide.region_12.13_spmd.clone, body=%wide.region_7.0_spmd.clone.sunk | while | flops 4851637248 | bytes 37959000 | solution.py:102
  138.4 22.2 %conditional.3 = ((f32[2,6,256]{2,1,0:T(8,128)S(1)}, f32[2,6,256]{2,1,0:T(8,128)S(1)}, f32[2,6,256,128]{3,2,1,0:T(8,128)})) conditional(s32[]{:T(128)} %convert_element_type.10, (f32[2,6,256]{2,1,0:T(8,128)S(1)}, f32[2,6,256]{2,1,0:T(8,128)S(1)}, f32[2,6,256,128]{3,2,1,0:T(8,128)}) %tuple.98, (s32[]{:T(128)}, s32[512]{0:T(512)S(1)}, s32[]{:T(128)}, ...), branch_computations={%region_8.8_spmd, %region_9.11_spmd} | conditional | flops 4851637248 | bytes 37955680 | solution.py:99
  138.7 7.0 %fusion.2 = (f32[2,6,256]{2,1,0:T(8,128)S(1)}, f32[2,512,256,6]{2,1,3,0:T(8,128)S(1)}) fusion(pred[256,512]{0,1:T(8,128)(4,1)S(1)} %broadcast_compare_fusion, f32[256,2,6,128]{3,0,2,1:T(8,128)S(1)} %get-tuple-element.399, f32[16,512,2,128]{3,1,2,0:T(8,128)} %get-tuple-element.397, s32[]{:T(128)} %get-tuple-element.398), kind=kOutput, calls=%fused_computation.3 | convolution fusion | flops 2420634624 | bytes 8532480 | tf_op jit(solution)/shard_map/while/body/eval_jaxpr/cond/branch_1_fun/tkgd,skd->kgts/dot_general | solution.py:50
  147.2 12.2 %multiply_add_fusion = f32[2,6,256,128]{3,2,1,0:T(8,128)S(1)} fusion(f32[2,6,256,128]{3,2,1,0:T(8,128)S(1)} %copy-done.2, f32[2,512,256,6]{2,1,3,0:T(8,128)S(1)} %get-tuple-element.535, f32[2,6,256]{2,1,0:T(8,128)S(1)} %max.6, pred[256,512]{0,1:T(8,128)(4,1)S(1)} %broadcast_compare_fusion, f32[2,6,256]{2,1,0:T(8,128)S(1)} %get-tuple-element.531, ...), kind=kOutput, calls=%fused_computation.11 | convolution fusion | flops 2422996992 | bytes 10117632 | tf_op jit(solution)/shard_map/while/body/eval_jaxpr/cond/branch_1_fun/kgts,skd->kgtd/dot_general | solution.py:57
  161.2 22.2 %conditional.3 = ((f32[2,6,256]{2,1,0:T(8,128)S(1)}, f32[2,6,256]{2,1,0:T(8,128)S(1)}, f32[2,6,256,128]{3,2,1,0:T(8,128)})) conditional(s32[]{:T(128)} %convert_element_type.10, (f32[2,6,256]{2,1,0:T(8,128)S(1)}, f32[2,6,256]{2,1,0:T(8,128)S(1)}, f32[2,6,256,128]{3,2,1,0:T(8,128)}) %tuple.98, (s32[]{:T(128)}, s32[512]{0:T(512)S(1)}, s32[]{:T(128)}, ...), branch_computations={%region_8.8_spmd, %region_9.11_spmd} | conditional | flops 4851637248 | bytes 37955680 | solution.py:99
  161.4 7.0 %fusion.2 = (f32[2,6,256]{2,1,0:T(8,128)S(1)}, f32[2,512,256,6]{2,1,3,0:T(8,128)S(1)}) fusion(pred[256,512]{0,1:T(8,128)(4,1)S(1)} %broadcast_compare_fusion, f32[256,2,6,128]{3,0,2,1:T(8,128)S(1)} %get-tuple-element.399, f32[16,512,2,128]{3,1,2,0:T(8,128)} %get-tuple-element.397, s32[]{:T(128)} %get-tuple-element.398), kind=kOutput, calls=%fused_computation.3 | convolution fusion | flops 2420634624 | bytes 8532480 | tf_op jit(solution)/shard_map/while/body/eval_jaxpr/cond/branch_1_fun/tkgd,skd->kgts/dot_general | solution.py:50
  170.0 12.2 %multiply_add_fusion = f32[2,6,256,128]{3,2,1,0:T(8,128)S(1)} fusion(f32[2,6,256,128]{3,2,1,0:T(8,128)S(1)} %copy-done.2, f32[2,512,256,6]{2,1,3,0:T(8,128)S(1)} %get-tuple-element.535, f32[2,6,256]{2,1,0:T(8,128)S(1)} %max.6, pred[256,512]{0,1:T(8,128)(4,1)S(1)} %broadcast_compare_fusion, f32[2,6,256]{2,1,0:T(8,128)S(1)} %get-tuple-element.531, ...), kind=kOutput, calls=%fused_computation.11 | convolution fusion | flops 2422996992 | bytes 10117632 | tf_op jit(solution)/shard_map/while/body/eval_jaxpr/cond/branch_1_fun/kgts,skd->kgtd/dot_general | solution.py:57
  183.9 22.2 %conditional.3 = ((f32[2,6,256]{2,1,0:T(8,128)S(1)}, f32[2,6,256]{2,1,0:T(8,128)S(1)}, f32[2,6,256,128]{3,2,1,0:T(8,128)})) conditional(s32[]{:T(128)} %convert_element_type.10, (f32[2,6,256]{2,1,0:T(8,128)S(1)}, f32[2,6,256]{2,1,0:T(8,128)S(1)}, f32[2,6,256,128]{3,2,1,0:T(8,128)}) %tuple.98, (s32[]{:T(128)}, s32[512]{0:T(512)S(1)}, s32[]{:T(128)}, ...), branch_computations={%region_8.8_spmd, %region_9.11_spmd} | conditional | flops 4851637248 | bytes 37955680 | solution.py:99
  184.1 7.0 %fusion.2 = (f32[2,6,256]{2,1,0:T(8,128)S(1)}, f32[2,512,256,6]{2,1,3,0:T(8,128)S(1)}) fusion(pred[256,512]{0,1:T(8,128)(4,1)S(1)} %broadcast_compare_fusion, f32[256,2,6,128]{3,0,2,1:T(8,128)S(1)} %get-tuple-element.399, f32[16,512,2,128]{3,1,2,0:T(8,128)} %get-tuple-element.397, s32[]{:T(128)} %get-tuple-element.398), kind=kOutput, calls=%fused_computation.3 | convolution fusion | flops 2420634624 | bytes 8532480 | tf_op jit(solution)/shard_map/while/body/eval_jaxpr/cond/branch_1_fun/tkgd,skd->kgts/dot_general | solution.py:50
  192.7 12.2 %multiply_add_fusion = f32[2,6,256,128]{3,2,1,0:T(8,128)S(1)} fusion(f32[2,6,256,128]{3,2,1,0:T(8,128)S(1)} %copy-done.2, f32[2,512,256,6]{2,1,3,0:T(8,128)S(1)} %get-tuple-element.535, f32[2,6,256]{2,1,0:T(8,128)S(1)} %max.6, pred[256,512]{0,1:T(8,128)(4,1)S(1)} %broadcast_compare_fusion, f32[2,6,256]{2,1,0:T(8,128)S(1)} %get-tuple-element.531, ...), kind=kOutput, calls=%fused_computation.11 | convolution fusion | flops 2422996992 | bytes 10117632 | tf_op jit(solution)/shard_map/while/body/eval_jaxpr/cond/branch_1_fun/kgts,skd->kgtd/dot_general | solution.py:57
  206.7 22.2 %conditional.3 = ((f32[2,6,256]{2,1,0:T(8,128)S(1)}, f32[2,6,256]{2,1,0:T(8,128)S(1)}, f32[2,6,256,128]{3,2,1,0:T(8,128)})) conditional(s32[]{:T(128)} %convert_element_type.10, (f32[2,6,256]{2,1,0:T(8,128)S(1)}, f32[2,6,256]{2,1,0:T(8,128)S(1)}, f32[2,6,256,128]{3,2,1,0:T(8,128)}) %tuple.98, (s32[]{:T(128)}, s32[512]{0:T(512)S(1)}, s32[]{:T(128)}, ...), branch_computations={%region_8.8_spmd, %region_9.11_spmd} | conditional | flops 4851637248 | bytes 37955680 | solution.py:99
  215.5 12.2 %multiply_add_fusion = f32[2,6,256,128]{3,2,1,0:T(8,128)S(1)} fusion(f32[2,6,256,128]{3,2,1,0:T(8,128)S(1)} %copy-done.2, f32[2,512,256,6]{2,1,3,0:T(8,128)S(1)} %get-tuple-element.535, f32[2,6,256]{2,1,0:T(8,128)S(1)} %max.6, pred[256,512]{0,1:T(8,128)(4,1)S(1)} %broadcast_compare_fusion, f32[2,6,256]{2,1,0:T(8,128)S(1)} %get-tuple-element.531, ...), kind=kOutput, calls=%fused_computation.11 | convolution fusion | flops 2422996992 | bytes 10117632 | tf_op jit(solution)/shard_map/while/body/eval_jaxpr/cond/branch_1_fun/kgts,skd->kgtd/dot_general | solution.py:57
  229.4 22.2 %conditional.3 = ((f32[2,6,256]{2,1,0:T(8,128)S(1)}, f32[2,6,256]{2,1,0:T(8,128)S(1)}, f32[2,6,256,128]{3,2,1,0:T(8,128)})) conditional(s32[]{:T(128)} %convert_element_type.10, (f32[2,6,256]{2,1,0:T(8,128)S(1)}, f32[2,6,256]{2,1,0:T(8,128)S(1)}, f32[2,6,256,128]{3,2,1,0:T(8,128)}) %tuple.98, (s32[]{:T(128)}, s32[512]{0:T(512)S(1)}, s32[]{:T(128)}, ...), branch_computations={%region_8.8_spmd, %region_9.11_spmd} | conditional | flops 4851637248 | bytes 37955680 | solution.py:99
  229.6 7.0 %fusion.2 = (f32[2,6,256]{2,1,0:T(8,128)S(1)}, f32[2,512,256,6]{2,1,3,0:T(8,128)S(1)}) fusion(pred[256,512]{0,1:T(8,128)(4,1)S(1)} %broadcast_compare_fusion, f32[256,2,6,128]{3,0,2,1:T(8,128)S(1)} %get-tuple-element.399, f32[16,512,2,128]{3,1,2,0:T(8,128)} %get-tuple-element.397, s32[]{:T(128)} %get-tuple-element.398), kind=kOutput, calls=%fused_computation.3 | convolution fusion | flops 2420634624 | bytes 8532480 | tf_op jit(solution)/shard_map/while/body/eval_jaxpr/cond/branch_1_fun/tkgd,skd->kgts/dot_general | solution.py:50
  238.2 12.2 %multiply_add_fusion = f32[2,6,256,128]{3,2,1,0:T(8,128)S(1)} fusion(f32[2,6,256,128]{3,2,1,0:T(8,128)S(1)} %copy-done.2, f32[2,512,256,6]{2,1,3,0:T(8,128)S(1)} %get-tuple-element.535, f32[2,6,256]{2,1,0:T(8,128)S(1)} %max.6, pred[256,512]{0,1:T(8,128)(4,1)S(1)} %broadcast_compare_fusion, f32[2,6,256]{2,1,0:T(8,128)S(1)} %get-tuple-element.531, ...), kind=kOutput, calls=%fused_computation.11 | convolution fusion | flops 2422996992 | bytes 10117632 | tf_op jit(solution)/shard_map/while/body/eval_jaxpr/cond/branch_1_fun/kgts,skd->kgtd/dot_general | solution.py:57
  252.2 22.2 %conditional.3 = ((f32[2,6,256]{2,1,0:T(8,128)S(1)}, f32[2,6,256]{2,1,0:T(8,128)S(1)}, f32[2,6,256,128]{3,2,1,0:T(8,128)})) conditional(s32[]{:T(128)} %convert_element_type.10, (f32[2,6,256]{2,1,0:T(8,128)S(1)}, f32[2,6,256]{2,1,0:T(8,128)S(1)}, f32[2,6,256,128]{3,2,1,0:T(8,128)}) %tuple.98, (s32[]{:T(128)}, s32[512]{0:T(512)S(1)}, s32[]{:T(128)}, ...), branch_computations={%region_8.8_spmd, %region_9.11_spmd} | conditional | flops 4851637248 | bytes 37955680 | solution.py:99
  261.0 12.2 %multiply_add_fusion = f32[2,6,256,128]{3,2,1,0:T(8,128)S(1)} fusion(f32[2,6,256,128]{3,2,1,0:T(8,128)S(1)} %copy-done.2, f32[2,512,256,6]{2,1,3,0:T(8,128)S(1)} %get-tuple-element.535, f32[2,6,256]{2,1,0:T(8,128)S(1)} %max.6, pred[256,512]{0,1:T(8,128)(4,1)S(1)} %broadcast_compare_fusion, f32[2,6,256]{2,1,0:T(8,128)S(1)} %get-tuple-element.531, ...), kind=kOutput, calls=%fused_computation.11 | convolution fusion | flops 2422996992 | bytes 10117632 | tf_op jit(solution)/shard_map/while/body/eval_jaxpr/cond/branch_1_fun/kgts,skd->kgtd/dot_general | solution.py:57
  274.9 22.2 %conditional.3 = ((f32[2,6,256]{2,1,0:T(8,128)S(1)}, f32[2,6,256]{2,1,0:T(8,128)S(1)}, f32[2,6,256,128]{3,2,1,0:T(8,128)})) conditional(s32[]{:T(128)} %convert_element_type.10, (f32[2,6,256]{2,1,0:T(8,128)S(1)}, f32[2,6,256]{2,1,0:T(8,128)S(1)}, f32[2,6,256,128]{3,2,1,0:T(8,128)}) %tuple.98, (s32[]{:T(128)}, s32[512]{0:T(512)S(1)}, s32[]{:T(128)}, ...), branch_computations={%region_8.8_spmd, %region_9.11_spmd} | conditional | flops 4851637248 | bytes 37955680 | solution.py:99
  275.1 7.0 %fusion.2 = (f32[2,6,256]{2,1,0:T(8,128)S(1)}, f32[2,512,256,6]{2,1,3,0:T(8,128)S(1)}) fusion(pred[256,512]{0,1:T(8,128)(4,1)S(1)} %broadcast_compare_fusion, f32[256,2,6,128]{3,0,2,1:T(8,128)S(1)} %get-tuple-element.399, f32[16,512,2,128]{3,1,2,0:T(8,128)} %get-tuple-element.397, s32[]{:T(128)} %get-tuple-element.398), kind=kOutput, calls=%fused_computation.3 | convolution fusion | flops 2420634624 | bytes 8532480 | tf_op jit(solution)/shard_map/while/body/eval_jaxpr/cond/branch_1_fun/tkgd,skd->kgts/dot_general | solution.py:50
  283.7 12.2 %multiply_add_fusion = f32[2,6,256,128]{3,2,1,0:T(8,128)S(1)} fusion(f32[2,6,256,128]{3,2,1,0:T(8,128)S(1)} %copy-done.2, f32[2,512,256,6]{2,1,3,0:T(8,128)S(1)} %get-tuple-element.535, f32[2,6,256]{2,1,0:T(8,128)S(1)} %max.6, pred[256,512]{0,1:T(8,128)(4,1)S(1)} %broadcast_compare_fusion, f32[2,6,256]{2,1,0:T(8,128)S(1)} %get-tuple-element.531, ...), kind=kOutput, calls=%fused_computation.11 | convolution fusion | flops 2422996992 | bytes 10117632 | tf_op jit(solution)/shard_map/while/body/eval_jaxpr/cond/branch_1_fun/kgts,skd->kgtd/dot_general | solution.py:57
  297.6 22.2 %conditional.3 = ((f32[2,6,256]{2,1,0:T(8,128)S(1)}, f32[2,6,256]{2,1,0:T(8,128)S(1)}, f32[2,6,256,128]{3,2,1,0:T(8,128)})) conditional(s32[]{:T(128)} %convert_element_type.10, (f32[2,6,256]{2,1,0:T(8,128)S(1)}, f32[2,6,256]{2,1,0:T(8,128)S(1)}, f32[2,6,256,128]{3,2,1,0:T(8,128)}) %tuple.98, (s32[]{:T(128)}, s32[512]{0:T(512)S(1)}, s32[]{:T(128)}, ...), branch_computations={%region_8.8_spmd, %region_9.11_spmd} | conditional | flops 4851637248 | bytes 37955680 | solution.py:99
  306.4 12.2 %multiply_add_fusion = f32[2,6,256,128]{3,2,1,0:T(8,128)S(1)} fusion(f32[2,6,256,128]{3,2,1,0:T(8,128)S(1)} %copy-done.2, f32[2,512,256,6]{2,1,3,0:T(8,128)S(1)} %get-tuple-element.535, f32[2,6,256]{2,1,0:T(8,128)S(1)} %max.6, pred[256,512]{0,1:T(8,128)(4,1)S(1)} %broadcast_compare_fusion, f32[2,6,256]{2,1,0:T(8,128)S(1)} %get-tuple-element.531, ...), kind=kOutput, calls=%fused_computation.11 | convolution fusion | flops 2422996992 | bytes 10117632 | tf_op jit(solution)/shard_map/while/body/eval_jaxpr/cond/branch_1_fun/kgts,skd->kgtd/dot_general | solution.py:57
  320.4 22.2 %conditional.3 = ((f32[2,6,256]{2,1,0:T(8,128)S(1)}, f32[2,6,256]{2,1,0:T(8,128)S(1)}, f32[2,6,256,128]{3,2,1,0:T(8,128)})) conditional(s32[]{:T(128)} %convert_element_type.10, (f32[2,6,256]{2,1,0:T(8,128)S(1)}, f32[2,6,256]{2,1,0:T(8,128)S(1)}, f32[2,6,256,128]{3,2,1,0:T(8,128)}) %tuple.98, (s32[]{:T(128)}, s32[512]{0:T(512)S(1)}, s32[]{:T(128)}, ...), branch_computations={%region_8.8_spmd, %region_9.11_spmd} | conditional | flops 4851637248 | bytes 37955680 | solution.py:99
  320.6 7.0 %fusion.2 = (f32[2,6,256]{2,1,0:T(8,128)S(1)}, f32[2,512,256,6]{2,1,3,0:T(8,128)S(1)}) fusion(pred[256,512]{0,1:T(8,128)(4,1)S(1)} %broadcast_compare_fusion, f32[256,2,6,128]{3,0,2,1:T(8,128)S(1)} %get-tuple-element.399, f32[16,512,2,128]{3,1,2,0:T(8,128)} %get-tuple-element.397, s32[]{:T(128)} %get-tuple-element.398), kind=kOutput, calls=%fused_computation.3 | convolution fusion | flops 2420634624 | bytes 8532480 | tf_op jit(solution)/shard_map/while/body/eval_jaxpr/cond/branch_1_fun/tkgd,skd->kgts/dot_general | solution.py:50
  329.2 12.2 %multiply_add_fusion = f32[2,6,256,128]{3,2,1,0:T(8,128)S(1)} fusion(f32[2,6,256,128]{3,2,1,0:T(8,128)S(1)} %copy-done.2, f32[2,512,256,6]{2,1,3,0:T(8,128)S(1)} %get-tuple-element.535, f32[2,6,256]{2,1,0:T(8,128)S(1)} %max.6, pred[256,512]{0,1:T(8,128)(4,1)S(1)} %broadcast_compare_fusion, f32[2,6,256]{2,1,0:T(8,128)S(1)} %get-tuple-element.531, ...), kind=kOutput, calls=%fused_computation.11 | convolution fusion | flops 2422996992 | bytes 10117632 | tf_op jit(solution)/shard_map/while/body/eval_jaxpr/cond/branch_1_fun/kgts,skd->kgtd/dot_general | solution.py:57
  343.1 22.2 %conditional.3 = ((f32[2,6,256]{2,1,0:T(8,128)S(1)}, f32[2,6,256]{2,1,0:T(8,128)S(1)}, f32[2,6,256,128]{3,2,1,0:T(8,128)})) conditional(s32[]{:T(128)} %convert_element_type.10, (f32[2,6,256]{2,1,0:T(8,128)S(1)}, f32[2,6,256]{2,1,0:T(8,128)S(1)}, f32[2,6,256,128]{3,2,1,0:T(8,128)}) %tuple.98, (s32[]{:T(128)}, s32[512]{0:T(512)S(1)}, s32[]{:T(128)}, ...), branch_computations={%region_8.8_spmd, %region_9.11_spmd} | conditional | flops 4851637248 | bytes 37955680 | solution.py:99
  351.9 12.2 %multiply_add_fusion = f32[2,6,256,128]{3,2,1,0:T(8,128)S(1)} fusion(f32[2,6,256,128]{3,2,1,0:T(8,128)S(1)} %copy-done.2, f32[2,512,256,6]{2,1,3,0:T(8,128)S(1)} %get-tuple-element.535, f32[2,6,256]{2,1,0:T(8,128)S(1)} %max.6, pred[256,512]{0,1:T(8,128)(4,1)S(1)} %broadcast_compare_fusion, f32[2,6,256]{2,1,0:T(8,128)S(1)} %get-tuple-element.531, ...), kind=kOutput, calls=%fused_computation.11 | convolution fusion | flops 2422996992 | bytes 10117632 | tf_op jit(solution)/shard_map/while/body/eval_jaxpr/cond/branch_1_fun/kgts,skd->kgtd/dot_general | solution.py:57
  365.9 22.2 %conditional.3 = ((f32[2,6,256]{2,1,0:T(8,128)S(1)}, f32[2,6,256]{2,1,0:T(8,128)S(1)}, f32[2,6,256,128]{3,2,1,0:T(8,128)})) conditional(s32[]{:T(128)} %convert_element_type.10, (f32[2,6,256]{2,1,0:T(8,128)S(1)}, f32[2,6,256]{2,1,0:T(8,128)S(1)}, f32[2,6,256,128]{3,2,1,0:T(8,128)}) %tuple.98, (s32[]{:T(128)}, s32[512]{0:T(512)S(1)}, s32[]{:T(128)}, ...), branch_computations={%region_8.8_spmd, %region_9.11_spmd} | conditional | flops 4851637248 | bytes 37955680 | solution.py:99
  366.1 7.0 %fusion.2 = (f32[2,6,256]{2,1,0:T(8,128)S(1)}, f32[2,512,256,6]{2,1,3,0:T(8,128)S(1)}) fusion(pred[256,512]{0,1:T(8,128)(4,1)S(1)} %broadcast_compare_fusion, f32[256,2,6,128]{3,0,2,1:T(8,128)S(1)} %get-tuple-element.399, f32[16,512,2,128]{3,1,2,0:T(8,128)} %get-tuple-element.397, s32[]{:T(128)} %get-tuple-element.398), kind=kOutput, calls=%fused_computation.3 | convolution fusion | flops 2420634624 | bytes 8532480 | tf_op jit(solution)/shard_map/while/body/eval_jaxpr/cond/branch_1_fun/tkgd,skd->kgts/dot_general | solution.py:50
  374.7 12.2 %multiply_add_fusion = f32[2,6,256,128]{3,2,1,0:T(8,128)S(1)} fusion(f32[2,6,256,128]{3,2,1,0:T(8,128)S(1)} %copy-done.2, f32[2,512,256,6]{2,1,3,0:T(8,128)S(1)} %get-tuple-element.535, f32[2,6,256]{2,1,0:T(8,128)S(1)} %max.6, pred[256,512]{0,1:T(8,128)(4,1)S(1)} %broadcast_compare_fusion, f32[2,6,256]{2,1,0:T(8,128)S(1)} %get-tuple-element.531, ...), kind=kOutput, calls=%fused_computation.11 | convolution fusion | flops 2422996992 | bytes 10117632 | tf_op jit(solution)/shard_map/while/body/eval_jaxpr/cond/branch_1_fun/kgts,skd->kgtd/dot_general | solution.py:57
  388.6 22.2 %conditional.3 = ((f32[2,6,256]{2,1,0:T(8,128)S(1)}, f32[2,6,256]{2,1,0:T(8,128)S(1)}, f32[2,6,256,128]{3,2,1,0:T(8,128)})) conditional(s32[]{:T(128)} %convert_element_type.10, (f32[2,6,256]{2,1,0:T(8,128)S(1)}, f32[2,6,256]{2,1,0:T(8,128)S(1)}, f32[2,6,256,128]{3,2,1,0:T(8,128)}) %tuple.98, (s32[]{:T(128)}, s32[512]{0:T(512)S(1)}, s32[]{:T(128)}, ...), branch_computations={%region_8.8_spmd, %region_9.11_spmd} | conditional | flops 4851637248 | bytes 37955680 | solution.py:99
  397.4 12.2 %multiply_add_fusion = f32[2,6,256,128]{3,2,1,0:T(8,128)S(1)} fusion(f32[2,6,256,128]{3,2,1,0:T(8,128)S(1)} %copy-done.2, f32[2,512,256,6]{2,1,3,0:T(8,128)S(1)} %get-tuple-element.535, f32[2,6,256]{2,1,0:T(8,128)S(1)} %max.6, pred[256,512]{0,1:T(8,128)(4,1)S(1)} %broadcast_compare_fusion, f32[2,6,256]{2,1,0:T(8,128)S(1)} %get-tuple-element.531, ...), kind=kOutput, calls=%fused_computation.11 | convolution fusion | flops 2422996992 | bytes 10117632 | tf_op jit(solution)/shard_map/while/body/eval_jaxpr/cond/branch_1_fun/kgts,skd->kgtd/dot_general | solution.py:57
  411.3 22.2 %conditional.3 = ((f32[2,6,256]{2,1,0:T(8,128)S(1)}, f32[2,6,256]{2,1,0:T(8,128)S(1)}, f32[2,6,256,128]{3,2,1,0:T(8,128)})) conditional(s32[]{:T(128)} %convert_element_type.10, (f32[2,6,256]{2,1,0:T(8,128)S(1)}, f32[2,6,256]{2,1,0:T(8,128)S(1)}, f32[2,6,256,128]{3,2,1,0:T(8,128)}) %tuple.98, (s32[]{:T(128)}, s32[512]{0:T(512)S(1)}, s32[]{:T(128)}, ...), branch_computations={%region_8.8_spmd, %region_9.11_spmd} | conditional | flops 4851637248 | bytes 37955680 | solution.py:99
  420.1 12.2 %multiply_add_fusion = f32[2,6,256,128]{3,2,1,0:T(8,128)S(1)} fusion(f32[2,6,256,128]{3,2,1,0:T(8,128)S(1)} %copy-done.2, f32[2,512,256,6]{2,1,3,0:T(8,128)S(1)} %get-tuple-element.535, f32[2,6,256]{2,1,0:T(8,128)S(1)} %max.6, pred[256,512]{0,1:T(8,128)(4,1)S(1)} %broadcast_compare_fusion, f32[2,6,256]{2,1,0:T(8,128)S(1)} %get-tuple-element.531, ...), kind=kOutput, calls=%fused_computation.11 | convolution fusion | flops 2422996992 | bytes 10117632 | tf_op jit(solution)/shard_map/while/body/eval_jaxpr/cond/branch_1_fun/kgts,skd->kgtd/dot_general | solution.py:57
  434.1 22.2 %conditional.3 = ((f32[2,6,256]{2,1,0:T(8,128)S(1)}, f32[2,6,256]{2,1,0:T(8,128)S(1)}, f32[2,6,256,128]{3,2,1,0:T(8,128)})) conditional(s32[]{:T(128)} %convert_element_type.10, (f32[2,6,256]{2,1,0:T(8,128)S(1)}, f32[2,6,256]{2,1,0:T(8,128)S(1)}, f32[2,6,256,128]{3,2,1,0:T(8,128)}) %tuple.98, (s32[]{:T(128)}, s32[512]{0:T(512)S(1)}, s32[]{:T(128)}, ...), branch_computations={%region_8.8_spmd, %region_9.11_spmd} | conditional | flops 4851637248 | bytes 37955680 | solution.py:99
  442.9 12.2 %multiply_add_fusion = f32[2,6,256,128]{3,2,1,0:T(8,128)S(1)} fusion(f32[2,6,256,128]{3,2,1,0:T(8,128)S(1)} %copy-done.2, f32[2,512,256,6]{2,1,3,0:T(8,128)S(1)} %get-tuple-element.535, f32[2,6,256]{2,1,0:T(8,128)S(1)} %max.6, pred[256,512]{0,1:T(8,128)(4,1)S(1)} %broadcast_compare_fusion, f32[2,6,256]{2,1,0:T(8,128)S(1)} %get-tuple-element.531, ...), kind=kOutput, calls=%fused_computation.11 | convolution fusion | flops 2422996992 | bytes 10117632 | tf_op jit(solution)/shard_map/while/body/eval_jaxpr/cond/branch_1_fun/kgts,skd->kgtd/dot_general | solution.py:57
  456.8 22.2 %conditional.3 = ((f32[2,6,256]{2,1,0:T(8,128)S(1)}, f32[2,6,256]{2,1,0:T(8,128)S(1)}, f32[2,6,256,128]{3,2,1,0:T(8,128)})) conditional(s32[]{:T(128)} %convert_element_type.10, (f32[2,6,256]{2,1,0:T(8,128)S(1)}, f32[2,6,256]{2,1,0:T(8,128)S(1)}, f32[2,6,256,128]{3,2,1,0:T(8,128)}) %tuple.98, (s32[]{:T(128)}, s32[512]{0:T(512)S(1)}, s32[]{:T(128)}, ...), branch_computations={%region_8.8_spmd, %region_9.11_spmd} | conditional | flops 4851637248 | bytes 37955680 | solution.py:99
  465.6 12.2 %multiply_add_fusion = f32[2,6,256,128]{3,2,1,0:T(8,128)S(1)} fusion(f32[2,6,256,128]{3,2,1,0:T(8,128)S(1)} %copy-done.2, f32[2,512,256,6]{2,1,3,0:T(8,128)S(1)} %get-tuple-element.535, f32[2,6,256]{2,1,0:T(8,128)S(1)} %max.6, pred[256,512]{0,1:T(8,128)(4,1)S(1)} %broadcast_compare_fusion, f32[2,6,256]{2,1,0:T(8,128)S(1)} %get-tuple-element.531, ...), kind=kOutput, calls=%fused_computation.11 | convolution fusion | flops 2422996992 | bytes 10117632 | tf_op jit(solution)/shard_map/while/body/eval_jaxpr/cond/branch_1_fun/kgts,skd->kgtd/dot_general | solution.py:57
  479.6 22.2 %conditional.3 = ((f32[2,6,256]{2,1,0:T(8,128)S(1)}, f32[2,6,256]{2,1,0:T(8,128)S(1)}, f32[2,6,256,128]{3,2,1,0:T(8,128)})) conditional(s32[]{:T(128)} %convert_element_type.10, (f32[2,6,256]{2,1,0:T(8,128)S(1)}, f32[2,6,256]{2,1,0:T(8,128)S(1)}, f32[2,6,256,128]{3,2,1,0:T(8,128)}) %tuple.98, (s32[]{:T(128)}, s32[512]{0:T(512)S(1)}, s32[]{:T(128)}, ...), branch_computations={%region_8.8_spmd, %region_9.11_spmd} | conditional | flops 4851637248 | bytes 37955680 | solution.py:99
  488.4 12.2 %multiply_add_fusion = f32[2,6,256,128]{3,2,1,0:T(8,128)S(1)} fusion(f32[2,6,256,128]{3,2,1,0:T(8,128)S(1)} %copy-done.2, f32[2,512,256,6]{2,1,3,0:T(8,128)S(1)} %get-tuple-element.535, f32[2,6,256]{2,1,0:T(8,128)S(1)} %max.6, pred[256,512]{0,1:T(8,128)(4,1)S(1)} %broadcast_compare_fusion, f32[2,6,256]{2,1,0:T(8,128)S(1)} %get-tuple-element.531, ...), kind=kOutput, calls=%fused_computation.11 | convolution fusion | flops 2422996992 | bytes 10117632 | tf_op jit(solution)/shard_map/while/body/eval_jaxpr/cond/branch_1_fun/kgts,skd->kgtd/dot_general | solution.py:57
  508.1 38.9 %while.34 = (s32[]{:T(128)}, f32[8,128,128]{2,1,0:T(8,128)S(1)}, s32[]{:T(128)}, f32[32,8]{1,0:T(8,128)S(1)}, f32[32,8,128,128]{3,2,1,0:T(8,128)}, /*index=5*/s32[]{:T(128)}, s32[]{:T(128)}) while((s32[]{:T(128)}, f32[8,128,128]{2,1,0:T(8,128)S(1)}, s32[]{:T(128)}, f32[32,8]{1,0:T(8,128)S(1)}, f32[32,8,128,128]{3,2,1,0:T(8,128)}, ...), condition=%wide.region_3.4_spmd.clone, body=%wide.region_2.3_spmd.clone.sunk | while | flops 524292 | bytes 1573065 | solution.py:28
  554.7 10.7 %psum.7 = f32[256,1]{0,1:T(1,128)S(1)} all-reduce(f32[256,1]{0,1:T(1,128)S(1)} %bitcast.97), channel_id=1, replica_groups=mesh['ctx'=32,'head'=4] {'head'}, use_global_device_ids=true, to_apply=%region_5.6 | all-reduce | flops 256 | bytes 2048 | tf_op jit(solution)/shard_map/psum | solution.py:131
  (327 shorter events, 182.5 us)
Async XLA Ops:
  7.2 75.3 %copy-start = (f32[256,1024]{1,0:T(8,128)S(1)}, f32[256,1024]{1,0:T(8,128)}, u32[]{:S(2)}) copy-start(f32[256,1024]{1,0:T(8,128)} %param.14) | copy-start | bytes 3145732
  7.2 79.7 %all-gather.6.cloned.1.call-start = ((), (), s32[]{:S(2)}) async-start(), calls=%async_computation | async-start | bytes 8650752 | tf_op jit(solution)/shard_map/all_gather | solution.py:76
  7.9 110.0 %all-gather.8.cloned.1.call-start = ((), (), s32[]{:S(2)}) async-start(), calls=%async_computation.1 | async-start | bytes 8650752 | tf_op jit(solution)/shard_map/all_gather | solution.py:77
  8.7 499.4 %all-gather.10.cloned.1.call-start = ((), (), s32[]{:S(2)}) async-start(), calls=%async_computation.2 | async-start | bytes 17301504 | tf_op jit(solution)/shard_map/all_gather | solution.py:16
  11.7 3.6 copy-start.1
  138.6 8.6 %copy-start.2 = (f32[2,6,256,128]{3,2,1,0:T(8,128)S(1)}, f32[2,6,256,128]{3,2,1,0:T(8,128)}, u32[]{:S(2)}) copy-start(f32[2,6,256,128]{3,2,1,0:T(8,128)} %get-tuple-element.401) | copy-start | bytes 4718596 | tf_op jit(solution)/shard_map/while/body/eval_jaxpr/cond
  159.5 1.1 copy-start.3
  161.4 8.6 %copy-start.2 = (f32[2,6,256,128]{3,2,1,0:T(8,128)S(1)}, f32[2,6,256,128]{3,2,1,0:T(8,128)}, u32[]{:S(2)}) copy-start(f32[2,6,256,128]{3,2,1,0:T(8,128)} %get-tuple-element.401) | copy-start | bytes 4718596 | tf_op jit(solution)/shard_map/while/body/eval_jaxpr/cond
  182.2 1.1 copy-start.3
  184.1 8.6 %copy-start.2 = (f32[2,6,256,128]{3,2,1,0:T(8,128)S(1)}, f32[2,6,256,128]{3,2,1,0:T(8,128)}, u32[]{:S(2)}) copy-start(f32[2,6,256,128]{3,2,1,0:T(8,128)} %get-tuple-element.401) | copy-start | bytes 4718596 | tf_op jit(solution)/shard_map/while/body/eval_jaxpr/cond
  205.0 1.1 copy-start.3
  206.9 8.6 %copy-start.2 = (f32[2,6,256,128]{3,2,1,0:T(8,128)S(1)}, f32[2,6,256,128]{3,2,1,0:T(8,128)}, u32[]{:S(2)}) copy-start(f32[2,6,256,128]{3,2,1,0:T(8,128)} %get-tuple-element.401) | copy-start | bytes 4718596 | tf_op jit(solution)/shard_map/while/body/eval_jaxpr/cond
  227.7 1.1 copy-start.3
  229.6 8.6 %copy-start.2 = (f32[2,6,256,128]{3,2,1,0:T(8,128)S(1)}, f32[2,6,256,128]{3,2,1,0:T(8,128)}, u32[]{:S(2)}) copy-start(f32[2,6,256,128]{3,2,1,0:T(8,128)} %get-tuple-element.401) | copy-start | bytes 4718596 | tf_op jit(solution)/shard_map/while/body/eval_jaxpr/cond
  250.4 1.1 copy-start.3
  252.4 8.6 %copy-start.2 = (f32[2,6,256,128]{3,2,1,0:T(8,128)S(1)}, f32[2,6,256,128]{3,2,1,0:T(8,128)}, u32[]{:S(2)}) copy-start(f32[2,6,256,128]{3,2,1,0:T(8,128)} %get-tuple-element.401) | copy-start | bytes 4718596 | tf_op jit(solution)/shard_map/while/body/eval_jaxpr/cond
  273.2 1.1 copy-start.3
  275.1 8.6 %copy-start.2 = (f32[2,6,256,128]{3,2,1,0:T(8,128)S(1)}, f32[2,6,256,128]{3,2,1,0:T(8,128)}, u32[]{:S(2)}) copy-start(f32[2,6,256,128]{3,2,1,0:T(8,128)} %get-tuple-element.401) | copy-start | bytes 4718596 | tf_op jit(solution)/shard_map/while/body/eval_jaxpr/cond
  295.9 1.1 copy-start.3
  297.8 8.6 %copy-start.2 = (f32[2,6,256,128]{3,2,1,0:T(8,128)S(1)}, f32[2,6,256,128]{3,2,1,0:T(8,128)}, u32[]{:S(2)}) copy-start(f32[2,6,256,128]{3,2,1,0:T(8,128)} %get-tuple-element.401) | copy-start | bytes 4718596 | tf_op jit(solution)/shard_map/while/body/eval_jaxpr/cond
  318.7 1.1 copy-start.3
  320.6 8.6 %copy-start.2 = (f32[2,6,256,128]{3,2,1,0:T(8,128)S(1)}, f32[2,6,256,128]{3,2,1,0:T(8,128)}, u32[]{:S(2)}) copy-start(f32[2,6,256,128]{3,2,1,0:T(8,128)} %get-tuple-element.401) | copy-start | bytes 4718596 | tf_op jit(solution)/shard_map/while/body/eval_jaxpr/cond
  341.4 1.1 copy-start.3
  343.3 8.6 %copy-start.2 = (f32[2,6,256,128]{3,2,1,0:T(8,128)S(1)}, f32[2,6,256,128]{3,2,1,0:T(8,128)}, u32[]{:S(2)}) copy-start(f32[2,6,256,128]{3,2,1,0:T(8,128)} %get-tuple-element.401) | copy-start | bytes 4718596 | tf_op jit(solution)/shard_map/while/body/eval_jaxpr/cond
  364.1 1.1 copy-start.3
  366.1 8.6 %copy-start.2 = (f32[2,6,256,128]{3,2,1,0:T(8,128)S(1)}, f32[2,6,256,128]{3,2,1,0:T(8,128)}, u32[]{:S(2)}) copy-start(f32[2,6,256,128]{3,2,1,0:T(8,128)} %get-tuple-element.401) | copy-start | bytes 4718596 | tf_op jit(solution)/shard_map/while/body/eval_jaxpr/cond
  386.9 1.1 copy-start.3
  388.8 8.6 %copy-start.2 = (f32[2,6,256,128]{3,2,1,0:T(8,128)S(1)}, f32[2,6,256,128]{3,2,1,0:T(8,128)}, u32[]{:S(2)}) copy-start(f32[2,6,256,128]{3,2,1,0:T(8,128)} %get-tuple-element.401) | copy-start | bytes 4718596 | tf_op jit(solution)/shard_map/while/body/eval_jaxpr/cond
  409.6 1.1 copy-start.3
  411.5 8.6 %copy-start.2 = (f32[2,6,256,128]{3,2,1,0:T(8,128)S(1)}, f32[2,6,256,128]{3,2,1,0:T(8,128)}, u32[]{:S(2)}) copy-start(f32[2,6,256,128]{3,2,1,0:T(8,128)} %get-tuple-element.401) | copy-start | bytes 4718596 | tf_op jit(solution)/shard_map/while/body/eval_jaxpr/cond
  432.4 1.1 copy-start.3
  434.3 8.6 %copy-start.2 = (f32[2,6,256,128]{3,2,1,0:T(8,128)S(1)}, f32[2,6,256,128]{3,2,1,0:T(8,128)}, u32[]{:S(2)}) copy-start(f32[2,6,256,128]{3,2,1,0:T(8,128)} %get-tuple-element.401) | copy-start | bytes 4718596 | tf_op jit(solution)/shard_map/while/body/eval_jaxpr/cond
  455.1 1.1 copy-start.3
  457.0 8.6 %copy-start.2 = (f32[2,6,256,128]{3,2,1,0:T(8,128)S(1)}, f32[2,6,256,128]{3,2,1,0:T(8,128)}, u32[]{:S(2)}) copy-start(f32[2,6,256,128]{3,2,1,0:T(8,128)} %get-tuple-element.401) | copy-start | bytes 4718596 | tf_op jit(solution)/shard_map/while/body/eval_jaxpr/cond
  477.9 1.1 copy-start.3
  479.8 8.6 %copy-start.2 = (f32[2,6,256,128]{3,2,1,0:T(8,128)S(1)}, f32[2,6,256,128]{3,2,1,0:T(8,128)}, u32[]{:S(2)}) copy-start(f32[2,6,256,128]{3,2,1,0:T(8,128)} %get-tuple-element.401) | copy-start | bytes 4718596 | tf_op jit(solution)/shard_map/while/body/eval_jaxpr/cond
  500.6 1.1 copy-start.3
  505.0 43.1 %copy-start.4 = (f32[256,1024]{1,0:T(8,128)S(1)}, f32[256,1024]{1,0:T(8,128)}, u32[]{:S(2)}) copy-start(f32[256,1024]{1,0:T(8,128)} %param.16) | copy-start | bytes 3145732
  546.9 18.5 %copy-start.5 = (f32[1024]{0:T(1024)S(1)}, f32[1024]{0:T(1024)}, u32[]{:S(2)}) copy-start(f32[1024]{0:T(1024)} %param.18) | copy-start | bytes 12292
Sparse Core Ops, SparseCore 0:
  10.3 52.9 all-gather.5
  65.5 52.3 all-gather.7
  120.2 71.9 all-gather.9
where the time goes:
time: 577 us; the launch traced here: 573 us
  matrix products  322 us (56%)
  local copies, waits for them, and re-layouts  72.5 us (13%)
  blocking collectives  69.9 us (12%)
  other arithmetic  68.9 us (12%)
  between operations  14.5 us (3%)
  waiting for transfers between devices  13.6 us (2%)
  loops' own time  11.8 us (2%)
    dot_general x16, matrix products, attend(): jnp.einsum('kgts,skd->kgtd', weights, value_slab, precision=HIGHEST)  195 us
    dot_general x16, matrix products, attend(): jnp.einsum('tkgd,skd->kgts', query_rows, key_slab, precision=HIGHEST)  113 us
    unnamed x1, blocking collectives  59.2 us
    select_n x32, other arithmetic, turn(): return jax.tree.map(lambda a, b: jnp.where(reached, a, b), new, before)  37.5 us
    unnamed x16, local copies, waits for them, and re-layouts  25.6 us
    reduce_sum x16, other arithmetic, attend(): new_total = old_total * shrink + jnp.sum(weights, axis=3)  24 us
    cond x80, local copies, waits for them, and re-layouts  18.2 us
    all_gather x1, waiting for transfers between devices, soft_layer(): value_rows = lax.all_gather(v_soft, 'ctx', axis=0, tiled=True)  12.2 us
  transfers between devices with their start and end apart: 3, of which 1 were waited for; matrix products, arithmetic and copies ran while one was open for 69% of the time, Pallas kernels for 0%

commit v1 on v0

--- a/solution.py
+++ b/solution.py
@@ -74,7 +74,9 @@
         )
     initial = tuple(initial)
     key_rows = lax.all_gather(k_soft, "ctx", axis=0, tiled=True)
-    value_rows = lax.all_gather(v_soft, "ctx", axis=0, tiled=True)
+    value_rows = jnp.concatenate(
+        lax.all_to_all(jnp.stack([v_soft] * lax.axis_size("ctx")), "ctx", 0, 0), axis=0
+    )
     shard_rows = key_rows.shape[0]
     key_block = math.gcd(shard_rows, 512)
     key_rows = key_rows.reshape(shard_rows // key_block, key_block, kv_heads, HD)

time: 577 us -> 708 us (1.23)
  blocking collectives: 69.9 us -> 175 us
  local copies, waits for them, and re-layouts: 72.5 us -> 88.6 us
  waiting for transfers between devices: 13.6 us -> 0.7 us
  loops' own time: 11.8 us -> 24.7 us
  starting transfers between devices: 0.11 us -> 7.57 us
    unnamed x1, blocking collectives: 59.2 us -> 162 us
    another operation x1 -> x3, local copies, waits for them, and re-layouts: 0.01 us -> 13.9 us  [the longest x1 9.8 us: soft_layer(): value_rows.reshape(shard_rows // key_block, key_block, kv_heads, HD)]
    another operation x1, loops' own time: 9.08 us -> 22 us  [soft_layer(): finals = lax.fori_loop(0, shard_rows // key_block, visit, initial)]
    all_gather x1 -> x0, waiting for transfers between devices: 12.2 us -> none  [soft_layer(): value_rows = lax.all_gather(v_soft, 'ctx', axis=0, tiled=True)]
    all_to_all x0 -> x1, local copies, waits for them, and re-layouts: none -> 11.8 us  [soft_layer(): lax.all_to_all(jnp.stack([v_soft] * lax.axis_size('ctx')), 'ctx', 0, 0)]
    reshape x1 -> x0, local copies, waits for them, and re-layouts: 10.8 us -> none  [soft_layer(): value_rows.reshape(shard_rows // key_block, key_block, kv_heads, HD)]
    all_to_all x0 -> x1, starting transfers between devices: none -> 7.49 us  [soft_layer(): lax.all_to_all(jnp.stack([v_soft] * lax.axis_size('ctx')), 'ctx', 0, 0)]
    unnamed x16 -> x19, local copies, waits for them, and re-layouts: 25.6 us -> 28 us
  transfers between devices with their start and end apart: 3 -> 3, of which waited for: 1 -> 0; matrix products, arithmetic and copies ran while one was open for 69% -> 59% of each run, Pallas kernels for 0% -> 0%
where the time goes in v1:
time: 708 us; the launch traced here: 701 us
  matrix products  321 us (45%)
  blocking collectives  175 us (25%)
  local copies, waits for them, and re-layouts  88.6 us (13%)
  other arithmetic  68.9 us (10%)
  loops' own time  24.7 us (3%)
  between operations  15.1 us (2%)
  starting transfers between devices  7.57 us (1%)
    dot_general x16, matrix products, attend(): jnp.einsum('kgts,skd->kgtd', weights, value_slab, precision=HIGHEST)  195 us
    unnamed x1, blocking collectives  162 us
    dot_general x16, matrix products, attend(): jnp.einsum('tkgd,skd->kgts', query_rows, key_slab, precision=HIGHEST)  113 us
    select_n x32, other arithmetic, turn(): return jax.tree.map(lambda a, b: jnp.where(reached, a, b), new, before)  37.5 us
    unnamed x19, local copies, waits for them, and re-layouts  28 us
    reduce_sum x16, other arithmetic, attend(): new_total = old_total * shrink + jnp.sum(weights, axis=3)  24 us
    another operation x1, loops' own time, soft_layer(): finals = lax.fori_loop(0, shard_rows // key_block, visit, initial)  22 us
    cond x80, local copies, waits for them, and re-layouts  18.2 us
  transfers between devices with their start and end apart: 3, of which 0 were waited for; matrix products, arithmetic and copies ran while one was open for 59% of the time, Pallas kernels for 0%

profile of v1, /device:TPU:30, one launch (start us, length us, event | category | flops | bytes accessed | tf_op | source)
XLA Modules:
  0.0 701.4 jit_solution(17910923994871494626)
XLA Ops:
  19.8 7.5 %all-to-all-start = ((f32[32,256,256]{1,2,0:T(8,128)}), f32[32,256,256]{1,2,0:T(8,128)}, u32[]{:S(2)}, u32[]{:S(2)}) async-start(f32[32,256,256]{1,2,0:T(8,128)} %stack.2), calls=%async_computation | async-start | bytes 16777216 | tf_op jit(solution)/shard_map/all_to_all | solution.py:78
  28.8 162.5 %all-reduce = f32[256]{0:T(256)S(1)} all-reduce(f32[256]{0:T(256)S(1)} %dynamic-update-slice), channel_id=2, replica_groups=mesh['ctx'=32,'head'=4] {'ctx'}, use_global_device_ids=true, to_apply=%add | all-reduce | flops 256 | bytes 2048
  201.7 11.8 %copy.66 = f32[32,256,256]{1,0,2:T(8,128)} copy(f32[32,256,256]{1,2,0:T(8,128)} %all-to-all-done) | data formatting | bytes 16777216 | tf_op jit(solution)/shard_map/all_to_all | solution.py:78
  213.5 9.8 %reshape_reshape.3 = f32[16,512,2,128]{1,0,3,2:T(8,128)} reshape(f32[32,256,256]{1,0,2:T(8,128)} %copy.66) | data formatting | bytes 16777216 | tf_op jit(solution)/shard_map/reshape;reshape | solution.py:83
  223.3 10.1 %copy.69 = f32[16,512,2,128]{3,1,2,0:T(8,128)} copy(f32[16,512,2,128]{1,0,3,2:T(8,128)} %reshape_reshape.3) | data formatting | bytes 16777216
  233.3 10.8 %reshape.133 = f32[16,512,2,128]{3,2,1,0:T(2,128)} reshape(f32[8192,256]{1,0:T(8,128)} %all-gather.5.cloned.1.call-done) | data formatting | bytes 16777216 | tf_op jit(solution)/shard_map/reshape | solution.py:82
  244.1 7.7 %copy.67 = f32[16,512,2,128]{3,1,2,0:T(8,128)} copy(f32[16,512,2,128]{3,2,1,0:T(2,128)} %reshape.133) | data formatting | bytes 16777216
  253.0 376.8 %while.33 = (s32[]{:T(128)}, f32[2,6,256]{2,1,0:T(8,128)S(1)}, f32[2,6,256]{2,1,0:T(8,128)S(1)}, f32[2,6,256,128]{3,2,1,0:T(8,128)}, s32[]{:T(128)}, /*index=5*/...) while((s32[]{:T(128)}, f32[2,6,256]{2,1,0:T(8,128)S(1)}, ...), condition=%wide.region_12.13_spmd.clone, body=%wide.region_7.0_spmd.clone.sunk | while | flops 4851637248 | bytes 37959000 | solution.py:104
  266.4 22.2 %conditional.3 = ((f32[2,6,256]{2,1,0:T(8,128)S(1)}, f32[2,6,256]{2,1,0:T(8,128)S(1)}, f32[2,6,256,128]{3,2,1,0:T(8,128)})) conditional(s32[]{:T(128)} %convert_element_type.10, (f32[2,6,256]{2,1,0:T(8,128)S(1)}, f32[2,6,256]{2,1,0:T(8,128)S(1)}, f32[2,6,256,128]{3,2,1,0:T(8,128)}) %tuple.98, (s32[]{:T(128)}, s32[512]{0:T(512)S(1)}, s32[]{:T(128)}, ...), branch_computations={%region_8.8_spmd, %region_9.11_spmd} | conditional | flops 4851637248 | bytes 37955680 | solution.py:101
  275.2 12.2 %multiply_add_fusion = f32[2,6,256,128]{3,2,1,0:T(8,128)S(1)} fusion(f32[2,6,256,128]{3,2,1,0:T(8,128)S(1)} %copy-done.2, f32[2,512,256,6]{2,1,3,0:T(8,128)S(1)} %get-tuple-element.535, f32[2,6,256]{2,1,0:T(8,128)S(1)} %max.6, pred[256,512]{0,1:T(8,128)(4,1)S(1)} %broadcast_compare_fusion, f32[2,6,256]{2,1,0:T(8,128)S(1)} %get-tuple-element.531, ...), kind=kOutput, calls=%fused_computation.11 | convolution fusion | flops 2422996992 | bytes 10117632 | tf_op jit(solution)/shard_map/while/body/eval_jaxpr/cond/branch_1_fun/kgts,skd->kgtd/dot_general | solution.py:57
  289.1 22.2 %conditional.3 = ((f32[2,6,256]{2,1,0:T(8,128)S(1)}, f32[2,6,256]{2,1,0:T(8,128)S(1)}, f32[2,6,256,128]{3,2,1,0:T(8,128)})) conditional(s32[]{:T(128)} %convert_element_type.10, (f32[2,6,256]{2,1,0:T(8,128)S(1)}, f32[2,6,256]{2,1,0:T(8,128)S(1)}, f32[2,6,256,128]{3,2,1,0:T(8,128)}) %tuple.98, (s32[]{:T(128)}, s32[512]{0:T(512)S(1)}, s32[]{:T(128)}, ...), branch_computations={%region_8.8_spmd, %region_9.11_spmd} | conditional | flops 4851637248 | bytes 37955680 | solution.py:101
  289.3 7.0 %fusion.2 = (f32[2,6,256]{2,1,0:T(8,128)S(1)}, f32[2,512,256,6]{2,1,3,0:T(8,128)S(1)}) fusion(pred[256,512]{0,1:T(8,128)(4,1)S(1)} %broadcast_compare_fusion, f32[256,2,6,128]{3,0,2,1:T(8,128)S(1)} %get-tuple-element.399, f32[16,512,2,128]{3,1,2,0:T(8,128)} %get-tuple-element.397, s32[]{:T(128)} %get-tuple-element.398), kind=kOutput, calls=%fused_computation.3 | convolution fusion | flops 2420634624 | bytes 8532480 | tf_op jit(solution)/shard_map/while/body/eval_jaxpr/cond/branch_1_fun/tkgd,skd->kgts/dot_general | solution.py:50
  297.9 12.2 %multiply_add_fusion = f32[2,6,256,128]{3,2,1,0:T(8,128)S(1)} fusion(f32[2,6,256,128]{3,2,1,0:T(8,128)S(1)} %copy-done.2, f32[2,512,256,6]{2,1,3,0:T(8,128)S(1)} %get-tuple-element.535, f32[2,6,256]{2,1,0:T(8,128)S(1)} %max.6, pred[256,512]{0,1:T(8,128)(4,1)S(1)} %broadcast_compare_fusion, f32[2,6,256]{2,1,0:T(8,128)S(1)} %get-tuple-element.531, ...), kind=kOutput, calls=%fused_computation.11 | convolution fusion | flops 2422996992 | bytes 10117632 | tf_op jit(solution)/shard_map/while/body/eval_jaxpr/cond/branch_1_fun/kgts,skd->kgtd/dot_general | solution.py:57
  311.9 22.2 %conditional.3 = ((f32[2,6,256]{2,1,0:T(8,128)S(1)}, f32[2,6,256]{2,1,0:T(8,128)S(1)}, f32[2,6,256,128]{3,2,1,0:T(8,128)})) conditional(s32[]{:T(128)} %convert_element_type.10, (f32[2,6,256]{2,1,0:T(8,128)S(1)}, f32[2,6,256]{2,1,0:T(8,128)S(1)}, f32[2,6,256,128]{3,2,1,0:T(8,128)}) %tuple.98, (s32[]{:T(128)}, s32[512]{0:T(512)S(1)}, s32[]{:T(128)}, ...), branch_computations={%region_8.8_spmd, %region_9.11_spmd} | conditional | flops 4851637248 | bytes 37955680 | solution.py:101
  320.7 12.2 %multiply_add_fusion = f32[2,6,256,128]{3,2,1,0:T(8,128)S(1)} fusion(f32[2,6,256,128]{3,2,1,0:T(8,128)S(1)} %copy-done.2, f32[2,512,256,6]{2,1,3,0:T(8,128)S(1)} %get-tuple-element.535, f32[2,6,256]{2,1,0:T(8,128)S(1)} %max.6, pred[256,512]{0,1:T(8,128)(4,1)S(1)} %broadcast_compare_fusion, f32[2,6,256]{2,1,0:T(8,128)S(1)} %get-tuple-element.531, ...), kind=kOutput, calls=%fused_computation.11 | convolution fusion | flops 2422996992 | bytes 10117632 | tf_op jit(solution)/shard_map/while/body/eval_jaxpr/cond/branch_1_fun/kgts,skd->kgtd/dot_general | solution.py:57
  334.6 22.2 %conditional.3 = ((f32[2,6,256]{2,1,0:T(8,128)S(1)}, f32[2,6,256]{2,1,0:T(8,128)S(1)}, f32[2,6,256,128]{3,2,1,0:T(8,128)})) conditional(s32[]{:T(128)} %convert_element_type.10, (f32[2,6,256]{2,1,0:T(8,128)S(1)}, f32[2,6,256]{2,1,0:T(8,128)S(1)}, f32[2,6,256,128]{3,2,1,0:T(8,128)}) %tuple.98, (s32[]{:T(128)}, s32[512]{0:T(512)S(1)}, s32[]{:T(128)}, ...), branch_computations={%region_8.8_spmd, %region_9.11_spmd} | conditional | flops 4851637248 | bytes 37955680 | solution.py:101
  334.8 7.0 %fusion.2 = (f32[2,6,256]{2,1,0:T(8,128)S(1)}, f32[2,512,256,6]{2,1,3,0:T(8,128)S(1)}) fusion(pred[256,512]{0,1:T(8,128)(4,1)S(1)} %broadcast_compare_fusion, f32[256,2,6,128]{3,0,2,1:T(8,128)S(1)} %get-tuple-element.399, f32[16,512,2,128]{3,1,2,0:T(8,128)} %get-tuple-element.397, s32[]{:T(128)} %get-tuple-element.398), kind=kOutput, calls=%fused_computation.3 | convolution fusion | flops 2420634624 | bytes 8532480 | tf_op jit(solution)/shard_map/while/body/eval_jaxpr/cond/branch_1_fun/tkgd,skd->kgts/dot_general | solution.py:50
  343.4 12.2 %multiply_add_fusion = f32[2,6,256,128]{3,2,1,0:T(8,128)S(1)} fusion(f32[2,6,256,128]{3,2,1,0:T(8,128)S(1)} %copy-done.2, f32[2,512,256,6]{2,1,3,0:T(8,128)S(1)} %get-tuple-element.535, f32[2,6,256]{2,1,0:T(8,128)S(1)} %max.6, pred[256,512]{0,1:T(8,128)(4,1)S(1)} %broadcast_compare_fusion, f32[2,6,256]{2,1,0:T(8,128)S(1)} %get-tuple-element.531, ...), kind=kOutput, calls=%fused_computation.11 | convolution fusion | flops 2422996992 | bytes 10117632 | tf_op jit(solution)/shard_map/while/body/eval_jaxpr/cond/branch_1_fun/kgts,skd->kgtd/dot_general | solution.py:57
  357.4 22.2 %conditional.3 = ((f32[2,6,256]{2,1,0:T(8,128)S(1)}, f32[2,6,256]{2,1,0:T(8,128)S(1)}, f32[2,6,256,128]{3,2,1,0:T(8,128)})) conditional(s32[]{:T(128)} %convert_element_type.10, (f32[2,6,256]{2,1,0:T(8,128)S(1)}, f32[2,6,256]{2,1,0:T(8,128)S(1)}, f32[2,6,256,128]{3,2,1,0:T(8,128)}) %tuple.98, (s32[]{:T(128)}, s32[512]{0:T(512)S(1)}, s32[]{:T(128)}, ...), branch_computations={%region_8.8_spmd, %region_9.11_spmd} | conditional | flops 4851637248 | bytes 37955680 | solution.py:101
  357.6 7.0 %fusion.2 = (f32[2,6,256]{2,1,0:T(8,128)S(1)}, f32[2,512,256,6]{2,1,3,0:T(8,128)S(1)}) fusion(pred[256,512]{0,1:T(8,128)(4,1)S(1)} %broadcast_compare_fusion, f32[256,2,6,128]{3,0,2,1:T(8,128)S(1)} %get-tuple-element.399, f32[16,512,2,128]{3,1,2,0:T(8,128)} %get-tuple-element.397, s32[]{:T(128)} %get-tuple-element.398), kind=kOutput, calls=%fused_computation.3 | convolution fusion | flops 2420634624 | bytes 8532480 | tf_op jit(solution)/shard_map/while/body/eval_jaxpr/cond/branch_1_fun/tkgd,skd->kgts/dot_general | solution.py:50
  366.2 12.2 %multiply_add_fusion = f32[2,6,256,128]{3,2,1,0:T(8,128)S(1)} fusion(f32[2,6,256,128]{3,2,1,0:T(8,128)S(1)} %copy-done.2, f32[2,512,256,6]{2,1,3,0:T(8,128)S(1)} %get-tuple-element.535, f32[2,6,256]{2,1,0:T(8,128)S(1)} %max.6, pred[256,512]{0,1:T(8,128)(4,1)S(1)} %broadcast_compare_fusion, f32[2,6,256]{2,1,0:T(8,128)S(1)} %get-tuple-element.531, ...), kind=kOutput, calls=%fused_computation.11 | convolution fusion | flops 2422996992 | bytes 10117632 | tf_op jit(solution)/shard_map/while/body/eval_jaxpr/cond/branch_1_fun/kgts,skd->kgtd/dot_general | solution.py:57
  380.1 22.2 %conditional.3 = ((f32[2,6,256]{2,1,0:T(8,128)S(1)}, f32[2,6,256]{2,1,0:T(8,128)S(1)}, f32[2,6,256,128]{3,2,1,0:T(8,128)})) conditional(s32[]{:T(128)} %convert_element_type.10, (f32[2,6,256]{2,1,0:T(8,128)S(1)}, f32[2,6,256]{2,1,0:T(8,128)S(1)}, f32[2,6,256,128]{3,2,1,0:T(8,128)}) %tuple.98, (s32[]{:T(128)}, s32[512]{0:T(512)S(1)}, s32[]{:T(128)}, ...), branch_computations={%region_8.8_spmd, %region_9.11_spmd} | conditional | flops 4851637248 | bytes 37955680 | solution.py:101
  388.9 12.2 %multiply_add_fusion = f32[2,6,256,128]{3,2,1,0:T(8,128)S(1)} fusion(f32[2,6,256,128]{3,2,1,0:T(8,128)S(1)} %copy-done.2, f32[2,512,256,6]{2,1,3,0:T(8,128)S(1)} %get-tuple-element.535, f32[2,6,256]{2,1,0:T(8,128)S(1)} %max.6, pred[256,512]{0,1:T(8,128)(4,1)S(1)} %broadcast_compare_fusion, f32[2,6,256]{2,1,0:T(8,128)S(1)} %get-tuple-element.531, ...), kind=kOutput, calls=%fused_computation.11 | convolution fusion | flops 2422996992 | bytes 10117632 | tf_op jit(solution)/shard_map/while/body/eval_jaxpr/cond/branch_1_fun/kgts,skd->kgtd/dot_general | solution.py:57
  402.9 22.2 %conditional.3 = ((f32[2,6,256]{2,1,0:T(8,128)S(1)}, f32[2,6,256]{2,1,0:T(8,128)S(1)}, f32[2,6,256,128]{3,2,1,0:T(8,128)})) conditional(s32[]{:T(128)} %convert_element_type.10, (f32[2,6,256]{2,1,0:T(8,128)S(1)}, f32[2,6,256]{2,1,0:T(8,128)S(1)}, f32[2,6,256,128]{3,2,1,0:T(8,128)}) %tuple.98, (s32[]{:T(128)}, s32[512]{0:T(512)S(1)}, s32[]{:T(128)}, ...), branch_computations={%region_8.8_spmd, %region_9.11_spmd} | conditional | flops 4851637248 | bytes 37955680 | solution.py:101
  403.1 7.0 %fusion.2 = (f32[2,6,256]{2,1,0:T(8,128)S(1)}, f32[2,512,256,6]{2,1,3,0:T(8,128)S(1)}) fusion(pred[256,512]{0,1:T(8,128)(4,1)S(1)} %broadcast_compare_fusion, f32[256,2,6,128]{3,0,2,1:T(8,128)S(1)} %get-tuple-element.399, f32[16,512,2,128]{3,1,2,0:T(8,128)} %get-tuple-element.397, s32[]{:T(128)} %get-tuple-element.398), kind=kOutput, calls=%fused_computation.3 | convolution fusion | flops 2420634624 | bytes 8532480 | tf_op jit(solution)/shard_map/while/body/eval_jaxpr/cond/branch_1_fun/tkgd,skd->kgts/dot_general | solution.py:50
  411.7 12.2 %multiply_add_fusion = f32[2,6,256,128]{3,2,1,0:T(8,128)S(1)} fusion(f32[2,6,256,128]{3,2,1,0:T(8,128)S(1)} %copy-done.2, f32[2,512,256,6]{2,1,3,0:T(8,128)S(1)} %get-tuple-element.535, f32[2,6,256]{2,1,0:T(8,128)S(1)} %max.6, pred[256,512]{0,1:T(8,128)(4,1)S(1)} %broadcast_compare_fusion, f32[2,6,256]{2,1,0:T(8,128)S(1)} %get-tuple-element.531, ...), kind=kOutput, calls=%fused_computation.11 | convolution fusion | flops 2422996992 | bytes 10117632 | tf_op jit(solution)/shard_map/while/body/eval_jaxpr/cond/branch_1_fun/kgts,skd->kgtd/dot_general | solution.py:57
  425.6 22.2 %conditional.3 = ((f32[2,6,256]{2,1,0:T(8,128)S(1)}, f32[2,6,256]{2,1,0:T(8,128)S(1)}, f32[2,6,256,128]{3,2,1,0:T(8,128)})) conditional(s32[]{:T(128)} %convert_element_type.10, (f32[2,6,256]{2,1,0:T(8,128)S(1)}, f32[2,6,256]{2,1,0:T(8,128)S(1)}, f32[2,6,256,128]{3,2,1,0:T(8,128)}) %tuple.98, (s32[]{:T(128)}, s32[512]{0:T(512)S(1)}, s32[]{:T(128)}, ...), branch_computations={%region_8.8_spmd, %region_9.11_spmd} | conditional | flops 4851637248 | bytes 37955680 | solution.py:101
  434.4 12.2 %multiply_add_fusion = f32[2,6,256,128]{3,2,1,0:T(8,128)S(1)} fusion(f32[2,6,256,128]{3,2,1,0:T(8,128)S(1)} %copy-done.2, f32[2,512,256,6]{2,1,3,0:T(8,128)S(1)} %get-tuple-element.535, f32[2,6,256]{2,1,0:T(8,128)S(1)} %max.6, pred[256,512]{0,1:T(8,128)(4,1)S(1)} %broadcast_compare_fusion, f32[2,6,256]{2,1,0:T(8,128)S(1)} %get-tuple-element.531, ...), kind=kOutput, calls=%fused_computation.11 | convolution fusion | flops 2422996992 | bytes 10117632 | tf_op jit(solution)/shard_map/while/body/eval_jaxpr/cond/branch_1_fun/kgts,skd->kgtd/dot_general | solution.py:57
  448.4 22.2 %conditional.3 = ((f32[2,6,256]{2,1,0:T(8,128)S(1)}, f32[2,6,256]{2,1,0:T(8,128)S(1)}, f32[2,6,256,128]{3,2,1,0:T(8,128)})) conditional(s32[]{:T(128)} %convert_element_type.10, (f32[2,6,256]{2,1,0:T(8,128)S(1)}, f32[2,6,256]{2,1,0:T(8,128)S(1)}, f32[2,6,256,128]{3,2,1,0:T(8,128)}) %tuple.98, (s32[]{:T(128)}, s32[512]{0:T(512)S(1)}, s32[]{:T(128)}, ...), branch_computations={%region_8.8_spmd, %region_9.11_spmd} | conditional | flops 4851637248 | bytes 37955680 | solution.py:101
  457.2 12.2 %multiply_add_fusion = f32[2,6,256,128]{3,2,1,0:T(8,128)S(1)} fusion(f32[2,6,256,128]{3,2,1,0:T(8,128)S(1)} %copy-done.2, f32[2,512,256,6]{2,1,3,0:T(8,128)S(1)} %get-tuple-element.535, f32[2,6,256]{2,1,0:T(8,128)S(1)} %max.6, pred[256,512]{0,1:T(8,128)(4,1)S(1)} %broadcast_compare_fusion, f32[2,6,256]{2,1,0:T(8,128)S(1)} %get-tuple-element.531, ...), kind=kOutput, calls=%fused_computation.11 | convolution fusion | flops 2422996992 | bytes 10117632 | tf_op jit(solution)/shard_map/while/body/eval_jaxpr/cond/branch_1_fun/kgts,skd->kgtd/dot_general | solution.py:57
  471.1 22.2 %conditional.3 = ((f32[2,6,256]{2,1,0:T(8,128)S(1)}, f32[2,6,256]{2,1,0:T(8,128)S(1)}, f32[2,6,256,128]{3,2,1,0:T(8,128)})) conditional(s32[]{:T(128)} %convert_element_type.10, (f32[2,6,256]{2,1,0:T(8,128)S(1)}, f32[2,6,256]{2,1,0:T(8,128)S(1)}, f32[2,6,256,128]{3,2,1,0:T(8,128)}) %tuple.98, (s32[]{:T(128)}, s32[512]{0:T(512)S(1)}, s32[]{:T(128)}, ...), branch_computations={%region_8.8_spmd, %region_9.11_spmd} | conditional | flops 4851637248 | bytes 37955680 | solution.py:101
  471.3 7.0 %fusion.2 = (f32[2,6,256]{2,1,0:T(8,128)S(1)}, f32[2,512,256,6]{2,1,3,0:T(8,128)S(1)}) fusion(pred[256,512]{0,1:T(8,128)(4,1)S(1)} %broadcast_compare_fusion, f32[256,2,6,128]{3,0,2,1:T(8,128)S(1)} %get-tuple-element.399, f32[16,512,2,128]{3,1,2,0:T(8,128)} %get-tuple-element.397, s32[]{:T(128)} %get-tuple-element.398), kind=kOutput, calls=%fused_computation.3 | convolution fusion | flops 2420634624 | bytes 8532480 | tf_op jit(solution)/shard_map/while/body/eval_jaxpr/cond/branch_1_fun/tkgd,skd->kgts/dot_general | solution.py:50
  479.9 12.2 %multiply_add_fusion = f32[2,6,256,128]{3,2,1,0:T(8,128)S(1)} fusion(f32[2,6,256,128]{3,2,1,0:T(8,128)S(1)} %copy-done.2, f32[2,512,256,6]{2,1,3,0:T(8,128)S(1)} %get-tuple-element.535, f32[2,6,256]{2,1,0:T(8,128)S(1)} %max.6, pred[256,512]{0,1:T(8,128)(4,1)S(1)} %broadcast_compare_fusion, f32[2,6,256]{2,1,0:T(8,128)S(1)} %get-tuple-element.531, ...), kind=kOutput, calls=%fused_computation.11 | convolution fusion | flops 2422996992 | bytes 10117632 | tf_op jit(solution)/shard_map/while/body/eval_jaxpr/cond/branch_1_fun/kgts,skd->kgtd/dot_general | solution.py:57
  493.9 22.2 %conditional.3 = ((f32[2,6,256]{2,1,0:T(8,128)S(1)}, f32[2,6,256]{2,1,0:T(8,128)S(1)}, f32[2,6,256,128]{3,2,1,0:T(8,128)})) conditional(s32[]{:T(128)} %convert_element_type.10, (f32[2,6,256]{2,1,0:T(8,128)S(1)}, f32[2,6,256]{2,1,0:T(8,128)S(1)}, f32[2,6,256,128]{3,2,1,0:T(8,128)}) %tuple.98, (s32[]{:T(128)}, s32[512]{0:T(512)S(1)}, s32[]{:T(128)}, ...), branch_computations={%region_8.8_spmd, %region_9.11_spmd} | conditional | flops 4851637248 | bytes 37955680 | solution.py:101
  502.7 12.2 %multiply_add_fusion = f32[2,6,256,128]{3,2,1,0:T(8,128)S(1)} fusion(f32[2,6,256,128]{3,2,1,0:T(8,128)S(1)} %copy-done.2, f32[2,512,256,6]{2,1,3,0:T(8,128)S(1)} %get-tuple-element.535, f32[2,6,256]{2,1,0:T(8,128)S(1)} %max.6, pred[256,512]{0,1:T(8,128)(4,1)S(1)} %broadcast_compare_fusion, f32[2,6,256]{2,1,0:T(8,128)S(1)} %get-tuple-element.531, ...), kind=kOutput, calls=%fused_computation.11 | convolution fusion | flops 2422996992 | bytes 10117632 | tf_op jit(solution)/shard_map/while/body/eval_jaxpr/cond/branch_1_fun/kgts,skd->kgtd/dot_general | solution.py:57
  516.6 22.2 %conditional.3 = ((f32[2,6,256]{2,1,0:T(8,128)S(1)}, f32[2,6,256]{2,1,0:T(8,128)S(1)}, f32[2,6,256,128]{3,2,1,0:T(8,128)})) conditional(s32[]{:T(128)} %convert_element_type.10, (f32[2,6,256]{2,1,0:T(8,128)S(1)}, f32[2,6,256]{2,1,0:T(8,128)S(1)}, f32[2,6,256,128]{3,2,1,0:T(8,128)}) %tuple.98, (s32[]{:T(128)}, s32[512]{0:T(512)S(1)}, s32[]{:T(128)}, ...), branch_computations={%region_8.8_spmd, %region_9.11_spmd} | conditional | flops 4851637248 | bytes 37955680 | solution.py:101
  525.4 12.2 %multiply_add_fusion = f32[2,6,256,128]{3,2,1,0:T(8,128)S(1)} fusion(f32[2,6,256,128]{3,2,1,0:T(8,128)S(1)} %copy-done.2, f32[2,512,256,6]{2,1,3,0:T(8,128)S(1)} %get-tuple-element.535, f32[2,6,256]{2,1,0:T(8,128)S(1)} %max.6, pred[256,512]{0,1:T(8,128)(4,1)S(1)} %broadcast_compare_fusion, f32[2,6,256]{2,1,0:T(8,128)S(1)} %get-tuple-element.531, ...), kind=kOutput, calls=%fused_computation.11 | convolution fusion | flops 2422996992 | bytes 10117632 | tf_op jit(solution)/shard_map/while/body/eval_jaxpr/cond/branch_1_fun/kgts,skd->kgtd/dot_general | solution.py:57
  539.4 22.2 %conditional.3 = ((f32[2,6,256]{2,1,0:T(8,128)S(1)}, f32[2,6,256]{2,1,0:T(8,128)S(1)}, f32[2,6,256,128]{3,2,1,0:T(8,128)})) conditional(s32[]{:T(128)} %convert_element_type.10, (f32[2,6,256]{2,1,0:T(8,128)S(1)}, f32[2,6,256]{2,1,0:T(8,128)S(1)}, f32[2,6,256,128]{3,2,1,0:T(8,128)}) %tuple.98, (s32[]{:T(128)}, s32[512]{0:T(512)S(1)}, s32[]{:T(128)}, ...), branch_computations={%region_8.8_spmd, %region_9.11_spmd} | conditional | flops 4851637248 | bytes 37955680 | solution.py:101
  548.2 12.2 %multiply_add_fusion = f32[2,6,256,128]{3,2,1,0:T(8,128)S(1)} fusion(f32[2,6,256,128]{3,2,1,0:T(8,128)S(1)} %copy-done.2, f32[2,512,256,6]{2,1,3,0:T(8,128)S(1)} %get-tuple-element.535, f32[2,6,256]{2,1,0:T(8,128)S(1)} %max.6, pred[256,512]{0,1:T(8,128)(4,1)S(1)} %broadcast_compare_fusion, f32[2,6,256]{2,1,0:T(8,128)S(1)} %get-tuple-element.531, ...), kind=kOutput, calls=%fused_computation.11 | convolution fusion | flops 2422996992 | bytes 10117632 | tf_op jit(solution)/shard_map/while/body/eval_jaxpr/cond/branch_1_fun/kgts,skd->kgtd/dot_general | solution.py:57
  562.1 22.2 %conditional.3 = ((f32[2,6,256]{2,1,0:T(8,128)S(1)}, f32[2,6,256]{2,1,0:T(8,128)S(1)}, f32[2,6,256,128]{3,2,1,0:T(8,128)})) conditional(s32[]{:T(128)} %convert_element_type.10, (f32[2,6,256]{2,1,0:T(8,128)S(1)}, f32[2,6,256]{2,1,0:T(8,128)S(1)}, f32[2,6,256,128]{3,2,1,0:T(8,128)}) %tuple.98, (s32[]{:T(128)}, s32[512]{0:T(512)S(1)}, s32[]{:T(128)}, ...), branch_computations={%region_8.8_spmd, %region_9.11_spmd} | conditional | flops 4851637248 | bytes 37955680 | solution.py:101
  570.9 12.2 %multiply_add_fusion = f32[2,6,256,128]{3,2,1,0:T(8,128)S(1)} fusion(f32[2,6,256,128]{3,2,1,0:T(8,128)S(1)} %copy-done.2, f32[2,512,256,6]{2,1,3,0:T(8,128)S(1)} %get-tuple-element.535, f32[2,6,256]{2,1,0:T(8,128)S(1)} %max.6, pred[256,512]{0,1:T(8,128)(4,1)S(1)} %broadcast_compare_fusion, f32[2,6,256]{2,1,0:T(8,128)S(1)} %get-tuple-element.531, ...), kind=kOutput, calls=%fused_computation.11 | convolution fusion | flops 2422996992 | bytes 10117632 | tf_op jit(solution)/shard_map/while/body/eval_jaxpr/cond/branch_1_fun/kgts,skd->kgtd/dot_general | solution.py:57
  584.9 22.2 %conditional.3 = ((f32[2,6,256]{2,1,0:T(8,128)S(1)}, f32[2,6,256]{2,1,0:T(8,128)S(1)}, f32[2,6,256,128]{3,2,1,0:T(8,128)})) conditional(s32[]{:T(128)} %convert_element_type.10, (f32[2,6,256]{2,1,0:T(8,128)S(1)}, f32[2,6,256]{2,1,0:T(8,128)S(1)}, f32[2,6,256,128]{3,2,1,0:T(8,128)}) %tuple.98, (s32[]{:T(128)}, s32[512]{0:T(512)S(1)}, s32[]{:T(128)}, ...), branch_computations={%region_8.8_spmd, %region_9.11_spmd} | conditional | flops 4851637248 | bytes 37955680 | solution.py:101
  585.1 7.0 %fusion.2 = (f32[2,6,256]{2,1,0:T(8,128)S(1)}, f32[2,512,256,6]{2,1,3,0:T(8,128)S(1)}) fusion(pred[256,512]{0,1:T(8,128)(4,1)S(1)} %broadcast_compare_fusion, f32[256,2,6,128]{3,0,2,1:T(8,128)S(1)} %get-tuple-element.399, f32[16,512,2,128]{3,1,2,0:T(8,128)} %get-tuple-element.397, s32[]{:T(128)} %get-tuple-element.398), kind=kOutput, calls=%fused_computation.3 | convolution fusion | flops 2420634624 | bytes 8532480 | tf_op jit(solution)/shard_map/while/body/eval_jaxpr/cond/branch_1_fun/tkgd,skd->kgts/dot_general | solution.py:50
  593.7 12.2 %multiply_add_fusion = f32[2,6,256,128]{3,2,1,0:T(8,128)S(1)} fusion(f32[2,6,256,128]{3,2,1,0:T(8,128)S(1)} %copy-done.2, f32[2,512,256,6]{2,1,3,0:T(8,128)S(1)} %get-tuple-element.535, f32[2,6,256]{2,1,0:T(8,128)S(1)} %max.6, pred[256,512]{0,1:T(8,128)(4,1)S(1)} %broadcast_compare_fusion, f32[2,6,256]{2,1,0:T(8,128)S(1)} %get-tuple-element.531, ...), kind=kOutput, calls=%fused_computation.11 | convolution fusion | flops 2422996992 | bytes 10117632 | tf_op jit(solution)/shard_map/while/body/eval_jaxpr/cond/branch_1_fun/kgts,skd->kgtd/dot_general | solution.py:57
  607.7 22.2 %conditional.3 = ((f32[2,6,256]{2,1,0:T(8,128)S(1)}, f32[2,6,256]{2,1,0:T(8,128)S(1)}, f32[2,6,256,128]{3,2,1,0:T(8,128)})) conditional(s32[]{:T(128)} %convert_element_type.10, (f32[2,6,256]{2,1,0:T(8,128)S(1)}, f32[2,6,256]{2,1,0:T(8,128)S(1)}, f32[2,6,256,128]{3,2,1,0:T(8,128)}) %tuple.98, (s32[]{:T(128)}, s32[512]{0:T(512)S(1)}, s32[]{:T(128)}, ...), branch_computations={%region_8.8_spmd, %region_9.11_spmd} | conditional | flops 4851637248 | bytes 37955680 | solution.py:101
  616.4 12.2 %multiply_add_fusion = f32[2,6,256,128]{3,2,1,0:T(8,128)S(1)} fusion(f32[2,6,256,128]{3,2,1,0:T(8,128)S(1)} %copy-done.2, f32[2,512,256,6]{2,1,3,0:T(8,128)S(1)} %get-tuple-element.535, f32[2,6,256]{2,1,0:T(8,128)S(1)} %max.6, pred[256,512]{0,1:T(8,128)(4,1)S(1)} %broadcast_compare_fusion, f32[2,6,256]{2,1,0:T(8,128)S(1)} %get-tuple-element.531, ...), kind=kOutput, calls=%fused_computation.11 | convolution fusion | flops 2422996992 | bytes 10117632 | tf_op jit(solution)/shard_map/while/body/eval_jaxpr/cond/branch_1_fun/kgts,skd->kgtd/dot_general | solution.py:57
  636.2 38.9 %while.34 = (s32[]{:T(128)}, f32[8,128,128]{2,1,0:T(8,128)S(1)}, s32[]{:T(128)}, f32[32,8]{1,0:T(8,128)S(1)}, f32[32,8,128,128]{3,2,1,0:T(8,128)}, /*index=5*/s32[]{:T(128)}, s32[]{:T(128)}) while((s32[]{:T(128)}, f32[8,128,128]{2,1,0:T(8,128)S(1)}, s32[]{:T(128)}, f32[32,8]{1,0:T(8,128)S(1)}, f32[32,8,128,128]{3,2,1,0:T(8,128)}, ...), condition=%wide.region_3.4_spmd.clone, body=%wide.region_2.3_spmd.clone.sunk | while | flops 524292 | bytes 1573065 | solution.py:28
  680.6 12.6 %psum.7 = f32[256,1]{0,1:T(1,128)S(1)} all-reduce(f32[256,1]{0,1:T(1,128)S(1)} %bitcast.99), channel_id=1, replica_groups=mesh['ctx'=32,'head'=4] {'head'}, use_global_device_ids=true, to_apply=%region_5.6 | all-reduce | flops 256 | bytes 2048 | tf_op jit(solution)/shard_map/psum | solution.py:133
  (331 shorter events, 191.4 us)
Async XLA Ops:
  7.2 190.2 %copy-start = (f32[256,1024]{1,0:T(8,128)S(1)}, f32[256,1024]{1,0:T(8,128)}, u32[]{:S(2)}) copy-start(f32[256,1024]{1,0:T(8,128)} %param.14) | copy-start | bytes 3145732
  7.2 226.1 %all-gather.5.cloned.1.call-start = ((), (), s32[]{:S(2)}) async-start(), calls=%async_computation.1 | async-start | bytes 8650752 | tf_op jit(solution)/shard_map/all_gather | solution.py:76
  7.9 628.2 %all-gather.7.cloned.1.call-start = ((), (), s32[]{:S(2)}) async-start(), calls=%async_computation.2 | async-start | bytes 17301504 | tf_op jit(solution)/shard_map/all_gather | solution.py:16
  11.0 8.8 %copy-start.1 = (f32[256,1024]{0,1:T(8,128)}, f32[256,1024]{0,1:T(8,128)S(1)}, u32[]{:S(2)}) copy-start(f32[256,1024]{0,1:T(8,128)S(1)} %copy.78) | copy-start | bytes 3145732
  19.8 7.5 %copy-start.6 = (u32[128]{0:T(128)S(1)}, u32[128]{0:T(128)}, u32[]{:S(2)}) copy-start(u32[128]{0:T(128)} %constant.131) | copy-start | bytes 1540
  19.8 181.9 %all-to-all-start = ((f32[32,256,256]{1,2,0:T(8,128)}), f32[32,256,256]{1,2,0:T(8,128)}, u32[]{:S(2)}, u32[]{:S(2)}) async-start(f32[32,256,256]{1,2,0:T(8,128)} %stack.2), calls=%async_computation | async-start | bytes 16777216 | tf_op jit(solution)/shard_map/all_to_all | solution.py:78
  266.6 8.6 %copy-start.2 = (f32[2,6,256,128]{3,2,1,0:T(8,128)S(1)}, f32[2,6,256,128]{3,2,1,0:T(8,128)}, u32[]{:S(2)}) copy-start(f32[2,6,256,128]{3,2,1,0:T(8,128)} %get-tuple-element.401) | copy-start | bytes 4718596 | tf_op jit(solution)/shard_map/while/body/eval_jaxpr/cond
  287.4 1.1 copy-start.3
  289.3 8.6 %copy-start.2 = (f32[2,6,256,128]{3,2,1,0:T(8,128)S(1)}, f32[2,6,256,128]{3,2,1,0:T(8,128)}, u32[]{:S(2)}) copy-start(f32[2,6,256,128]{3,2,1,0:T(8,128)} %get-tuple-element.401) | copy-start | bytes 4718596 | tf_op jit(solution)/shard_map/while/body/eval_jaxpr/cond
  310.1 1.1 copy-start.3
  312.1 8.6 %copy-start.2 = (f32[2,6,256,128]{3,2,1,0:T(8,128)S(1)}, f32[2,6,256,128]{3,2,1,0:T(8,128)}, u32[]{:S(2)}) copy-start(f32[2,6,256,128]{3,2,1,0:T(8,128)} %get-tuple-element.401) | copy-start | bytes 4718596 | tf_op jit(solution)/shard_map/while/body/eval_jaxpr/cond
  332.9 1.1 copy-start.3
  334.8 8.6 %copy-start.2 = (f32[2,6,256,128]{3,2,1,0:T(8,128)S(1)}, f32[2,6,256,128]{3,2,1,0:T(8,128)}, u32[]{:S(2)}) copy-start(f32[2,6,256,128]{3,2,1,0:T(8,128)} %get-tuple-element.401) | copy-start | bytes 4718596 | tf_op jit(solution)/shard_map/while/body/eval_jaxpr/cond
  355.6 1.1 copy-start.3
  357.6 8.6 %copy-start.2 = (f32[2,6,256,128]{3,2,1,0:T(8,128)S(1)}, f32[2,6,256,128]{3,2,1,0:T(8,128)}, u32[]{:S(2)}) copy-start(f32[2,6,256,128]{3,2,1,0:T(8,128)} %get-tuple-element.401) | copy-start | bytes 4718596 | tf_op jit(solution)/shard_map/while/body/eval_jaxpr/cond
  378.4 1.1 copy-start.3
  380.3 8.6 %copy-start.2 = (f32[2,6,256,128]{3,2,1,0:T(8,128)S(1)}, f32[2,6,256,128]{3,2,1,0:T(8,128)}, u32[]{:S(2)}) copy-start(f32[2,6,256,128]{3,2,1,0:T(8,128)} %get-tuple-element.401) | copy-start | bytes 4718596 | tf_op jit(solution)/shard_map/while/body/eval_jaxpr/cond
  401.2 1.1 copy-start.3
  403.1 8.6 %copy-start.2 = (f32[2,6,256,128]{3,2,1,0:T(8,128)S(1)}, f32[2,6,256,128]{3,2,1,0:T(8,128)}, u32[]{:S(2)}) copy-start(f32[2,6,256,128]{3,2,1,0:T(8,128)} %get-tuple-element.401) | copy-start | bytes 4718596 | tf_op jit(solution)/shard_map/while/body/eval_jaxpr/cond
  423.9 1.1 copy-start.3
  425.8 8.6 %copy-start.2 = (f32[2,6,256,128]{3,2,1,0:T(8,128)S(1)}, f32[2,6,256,128]{3,2,1,0:T(8,128)}, u32[]{:S(2)}) copy-start(f32[2,6,256,128]{3,2,1,0:T(8,128)} %get-tuple-element.401) | copy-start | bytes 4718596 | tf_op jit(solution)/shard_map/while/body/eval_jaxpr/cond
  446.7 1.1 copy-start.3
  448.6 8.6 %copy-start.2 = (f32[2,6,256,128]{3,2,1,0:T(8,128)S(1)}, f32[2,6,256,128]{3,2,1,0:T(8,128)}, u32[]{:S(2)}) copy-start(f32[2,6,256,128]{3,2,1,0:T(8,128)} %get-tuple-element.401) | copy-start | bytes 4718596 | tf_op jit(solution)/shard_map/while/body/eval_jaxpr/cond
  469.4 1.1 copy-start.3
  471.3 8.6 %copy-start.2 = (f32[2,6,256,128]{3,2,1,0:T(8,128)S(1)}, f32[2,6,256,128]{3,2,1,0:T(8,128)}, u32[]{:S(2)}) copy-start(f32[2,6,256,128]{3,2,1,0:T(8,128)} %get-tuple-element.401) | copy-start | bytes 4718596 | tf_op jit(solution)/shard_map/while/body/eval_jaxpr/cond
  492.2 1.1 copy-start.3
  494.1 8.6 %copy-start.2 = (f32[2,6,256,128]{3,2,1,0:T(8,128)S(1)}, f32[2,6,256,128]{3,2,1,0:T(8,128)}, u32[]{:S(2)}) copy-start(f32[2,6,256,128]{3,2,1,0:T(8,128)} %get-tuple-element.401) | copy-start | bytes 4718596 | tf_op jit(solution)/shard_map/while/body/eval_jaxpr/cond
  514.9 1.1 copy-start.3
  516.8 8.6 %copy-start.2 = (f32[2,6,256,128]{3,2,1,0:T(8,128)S(1)}, f32[2,6,256,128]{3,2,1,0:T(8,128)}, u32[]{:S(2)}) copy-start(f32[2,6,256,128]{3,2,1,0:T(8,128)} %get-tuple-element.401) | copy-start | bytes 4718596 | tf_op jit(solution)/shard_map/while/body/eval_jaxpr/cond
  537.7 1.1 copy-start.3
  539.6 8.6 %copy-start.2 = (f32[2,6,256,128]{3,2,1,0:T(8,128)S(1)}, f32[2,6,256,128]{3,2,1,0:T(8,128)}, u32[]{:S(2)}) copy-start(f32[2,6,256,128]{3,2,1,0:T(8,128)} %get-tuple-element.401) | copy-start | bytes 4718596 | tf_op jit(solution)/shard_map/while/body/eval_jaxpr/cond
  560.4 1.1 copy-start.3
  562.3 8.6 %copy-start.2 = (f32[2,6,256,128]{3,2,1,0:T(8,128)S(1)}, f32[2,6,256,128]{3,2,1,0:T(8,128)}, u32[]{:S(2)}) copy-start(f32[2,6,256,128]{3,2,1,0:T(8,128)} %get-tuple-element.401) | copy-start | bytes 4718596 | tf_op jit(solution)/shard_map/while/body/eval_jaxpr/cond
  583.2 1.1 copy-start.3
  585.1 8.6 %copy-start.2 = (f32[2,6,256,128]{3,2,1,0:T(8,128)S(1)}, f32[2,6,256,128]{3,2,1,0:T(8,128)}, u32[]{:S(2)}) copy-start(f32[2,6,256,128]{3,2,1,0:T(8,128)} %get-tuple-element.401) | copy-start | bytes 4718596 | tf_op jit(solution)/shard_map/while/body/eval_jaxpr/cond
  605.9 1.1 copy-start.3
  607.8 8.6 %copy-start.2 = (f32[2,6,256,128]{3,2,1,0:T(8,128)S(1)}, f32[2,6,256,128]{3,2,1,0:T(8,128)}, u32[]{:S(2)}) copy-start(f32[2,6,256,128]{3,2,1,0:T(8,128)} %get-tuple-element.401) | copy-start | bytes 4718596 | tf_op jit(solution)/shard_map/while/body/eval_jaxpr/cond
  628.7 1.1 copy-start.3
  633.0 43.1 %copy-start.4 = (f32[256,1024]{1,0:T(8,128)S(1)}, f32[256,1024]{1,0:T(8,128)}, u32[]{:S(2)}) copy-start(f32[256,1024]{1,0:T(8,128)} %param.16) | copy-start | bytes 3145732
  675.0 18.2 %copy-start.5 = (f32[1024]{0:T(1024)S(1)}, f32[1024]{0:T(1024)}, u32[]{:S(2)}) copy-start(f32[1024]{0:T(1024)} %param.18) | copy-start | bytes 12292
Sparse Core Ops, SparseCore 0:
  10.3 129.2 all-gather.4
  141.8 74.4 all-gather.6
